TPU v7x, 128 devices: a whole 4x4x4 slice. The times are simulated.
128 devices in a mesh: wide: 8 (over x, core), narrow: 16 (over y, z).
Axes of the slice: x: 4, y: 4, z: 4, core: 2. Of those that a mesh axis runs over, the one named last changes fastest.
Arguments:
- blocks: float32 [5120, 256, 256], P(('wide', 'narrow'))
- block_map: int32 [5120, 2], P(('wide', 'narrow')), may hold values from 0 to 191, as said below
Outputs:
- factored: float32 [5120, 256, 256], P(('wide', 'narrow'))
Inputs may be any that keep to these rules, and one draw needn't show every extreme that they name: `block_map`: each row names a block (r, c) with r >= c, and no block is named twice. The device at wide index w and narrow index n holds only blocks with r equal to n modulo the size of narrow and c equal to w modulo the size of wide. Block column 0 and block column 1 are held at wide index 0 and 1, 4 blocks of them on each device there, in that device's first 4 slots in ascending r; block column 0 holds the block (1, 0).
All inputs are finite; a program needn't handle non-finite values.
Results may differ from a plain program's by a relative error of at most 0.00005.
Values sent between devices are 32-bit elements; how exact they have to be, the bound alone decides.
A program may use at most 128 MiB of HBM per device.

v0:
```python
import jax
import jax.numpy as jnp
from jax import lax
from jax.sharding import PartitionSpec as P

PR_DEV = 4


HIGHEST_PRECISION = lax.Precision.HIGHEST


def broadcast(x, axis, root):
    mine = lax.axis_index(axis) == root
    return lax.psum(jnp.where(mine, x, jnp.zeros_like(x)), axis)


def subtract_terms(current, selector, products):
    flat_products = products.reshape(-1, products.shape[-2] * products.shape[-1])
    removed = jnp.dot(
        selector, flat_products, precision=HIGHEST_PRECISION, preferred_element_type=jnp.float32
    )
    return current - removed.reshape(current.shape)


def factor_step(blocks, block_map, column):
    wide_index = lax.axis_index("wide")
    wide_count = lax.axis_size("wide")
    narrow_count = lax.axis_size("narrow")
    block_width = blocks.shape[1]
    rows_here = block_map[:, 0]
    cols_here = block_map[:, 1]
    diag_block = broadcast(blocks[0], "narrow", column)
    is_owner = wide_index == column
    pivot_block = jnp.where(is_owner, diag_block, jnp.eye(block_width, dtype=jnp.float32))
    lower_factor = jnp.linalg.cholesky(pivot_block)
    panel_old = blocks[:PR_DEV]
    stacked = jnp.transpose(panel_old, (2, 0, 1)).reshape(block_width, PR_DEV * block_width)
    solved = lax.linalg.triangular_solve(lower_factor, stacked, left_side=True, lower=True)
    solved = solved.reshape(block_width, PR_DEV, block_width).transpose(1, 2, 0)
    on_diag = (rows_here[:PR_DEV] == cols_here[:PR_DEV])[:, None, None]
    factored = jnp.where(on_diag, lower_factor[None], solved)
    panel_new = jnp.where(is_owner, factored, panel_old)
    blocks = jnp.concatenate([panel_new, blocks[PR_DEV:]], axis=0)
    row_blocks, row_ids = (
        broadcast(panel_new, "wide", column),
        broadcast(rows_here[:PR_DEV], "wide", column),
    )
    sources = narrow_count // wide_count
    every_block, every_id = (
        lax.all_gather(row_blocks, "narrow", axis=0, tiled=True),
        lax.all_gather(row_ids, "narrow", axis=0, tiled=True),
    )
    offsets = [(wide_index + source * wide_count) * PR_DEV for source in range(sources)]
    col_blocks = jnp.concatenate(
        [lax.dynamic_slice_in_dim(every_block, offset, PR_DEV, 0) for offset in offsets], axis=0
    )
    col_ids = jnp.concatenate(
        [lax.dynamic_slice_in_dim(every_id, offset, PR_DEV, 0) for offset in offsets], axis=0
    )
    products = jnp.einsum("iab,jcb->ijac", row_blocks, col_blocks, precision=HIGHEST_PRECISION)
    match_rows = rows_here[:, None] == row_ids[None, :]
    match_cols = cols_here[:, None] == col_ids[None, :]
    usable = ((rows_here > column) & (cols_here > column))[:, None, None]
    selector = (match_rows[:, :, None] & match_cols[:, None, :] & usable).astype(jnp.float32)
    selector = selector.reshape(rows_here.shape[0], -1)
    return (blocks, selector, products)


def on_device(blocks, block_map):
    blocks, selector, products = factor_step(blocks, block_map, 0)
    blocks = subtract_terms(blocks, selector, products)
    blocks, selector, products = factor_step(blocks, block_map, 1)
    return subtract_terms(blocks, selector, products)


def solution(mesh):
    return jax.shard_map(
        on_device,
        mesh=mesh,
        in_specs=(P(("wide", "narrow"), None, None), P(("wide", "narrow"), None)),
        out_specs=P(("wide", "narrow"), None, None),
        check_vma=False,
    )
```

profile of v0, /device:TPU:5, one launch (start us, length us, event | category | flops | bytes accessed | tf_op | source)
XLA Modules:
  0.0 793.4 jit_solution(6601698412776936651)
XLA Ops:
  8.5 1.3 slice.83
  11.1 84.9 %all-reduce.10.cloned.1.call-done = f32[256,256]{0,1:T(8,128)} async-done(((f32[256,256]{0,1:T(8,128)}), f32[256,256]{0,1:T(8,128)}) %all-reduce.10.cloned.1.call-update) | async-done | bytes 262160 | tf_op jit(solution)/shard_map/psum | solution.py:14
  96.3 11.7 %cholesky.130 = f32[128,128]{1,0:T(8,128)S(1)} custom-call(f32[128,128]{1,0:T(8,128)S(1)} %cholesky.194), custom_call_target="Cholesky" | custom-call | tf_op jit(solution)/shard_map/jit(cholesky)/cholesky | solution.py:35
  108.1 9.8 %custom-call.13 = f32[1,128,128]{1,2,0:T(8,128)S(1)} custom-call(f32[1,128,128]{2,1,0:T(8,128)S(1)} %get-tuple-element.66), custom_call_target="InvertDiagBlocksLowerTriangular" | custom-call | tf_op jit(solution)/shard_map/jit(cholesky)/cholesky | solution.py:35
  118.4 11.7 %cholesky.147 = f32[128,128]{1,0:T(8,128)S(1)} custom-call(f32[128,128]{1,0:T(8,128)S(1)} %convolution_subtract_fusion.3), custom_call_target="Cholesky" | custom-call | tf_op jit(solution)/shard_map/jit(cholesky)/cholesky | solution.py:35
  132.9 1.1 copy.43
  134.1 4.4 while.4
  135.0 1.4 bitcast_dynamic-update-slice_fusion.4
  137.1 1.4 bitcast_dynamic-update-slice_fusion.4
  138.5 19.7 %custom-call.14 = f32[2,128,128]{1,2,0:T(8,128)S(1)} custom-call(f32[2,128,128]{2,1,0:T(8,128)S(1)} %get-tuple-element.21), custom_call_target="InvertDiagBlocksLowerTriangular" | custom-call | tf_op jit(solution)/shard_map/triangular_solve/custom-call.0 | solution.py:38
  160.2 1.3 copy.47
  161.5 1.6 copy.48
  163.1 1.3 broadcast_select_fusion.1
  164.4 59.5 %all-reduce.12.cloned.1.call-done = f32[4,256,256]{1,2,0:T(8,128)} async-done(((f32[4,256,256]{1,2,0:T(8,128)}), f32[4,256,256]{1,2,0:T(8,128)}) %all-reduce.12.cloned.1.call-update) | async-done | bytes 1048592 | tf_op jit(solution)/shard_map/psum | solution.py:14
  223.9 2.5 copy.50
  226.5 6.8 all-reduce.4
  233.3 8.9 %slice.84 = f32[36,256,256]{2,1,0:T(8,128)} slice(f32[40,256,256]{2,1,0:T(8,128)} %param.5), slice={[4:40], [0:256], [0:256]} | slice | bytes 18874368 | tf_op jit(solution)/shard_map/slice | solution.py:43
  242.2 9.8 %copy.76 = f32[36,256,256]{1,2,0:T(8,128)} copy(f32[36,256,256]{2,1,0:T(8,128)} %slice.84) | data formatting | bytes 18874368
  253.7 13.2 %all-reduce.3 = (s32[64]{0:T(128)S(1)}, s32[64]{0:T(128)S(1)}) all-reduce(s32[64]{0:T(128)S(1)} %dynamic-update-slice.9, s32[64]{0:T(128)S(1)} %dynamic-update-slice.10), channel_id=1, replica_groups=mesh['wide'=8,'narrow'=16] {'narrow'}, use_global_device_ids=true, to_apply=%add.1 | all-reduce | flops 128 | bytes 1024
  267.3 73.6 %all-gather.3.cloned.1.call-done = f32[64,256,256]{2,1,0:T(8,128)} async-done(((f32[4,256,256]{2,1,0:T(8,128)}), f32[64,256,256]{2,1,0:T(8,128)}) %all-gather.3.cloned.1.call-update) | async-done | bytes 16777232 | tf_op jit(solution)/shard_map/all_gather | solution.py:50
  340.9 1.7 constant_dynamic-slice_fusion.5
  342.6 9.1 %convolution_bitcast_fusion.1 = f32[4,8,256,256]{2,3,0,1:T(8,128)} fusion(f32[4,256,256]{2,1,0:T(8,128)S(1)} %get-tuple-element.58, f32[4,256,256]{2,1,0:T(8,128)S(1)} %get-tuple-element.57, f32[4,256,256]{1,2,0:T(8,128)S(1)} %copy-done.1), kind=kOutput, calls=%fused_computation.13 | convolution fusion | flops 6442975232 | bytes 11534336 | tf_op jit(solution)/shard_map/iab,jcb->ijac/dot_general | solution.py:60
  351.6 10.4 %copy.82 = f32[4,8,256,256]{3,1,2,0:T(8,128)} copy(f32[4,8,256,256]{2,3,0,1:T(8,128)} %convolution_bitcast_fusion.1) | data formatting | bytes 16777216
  362.1 9.4 %fusion.3 = f32[40,256,256]{2,0,1:T(8,128)} fusion(pred[40]{0:T(512)(128)(4,1)S(1)} %get-tuple-element.68, pred[40,8]{0,1:T(8,128)(4,1)S(1)} %get-tuple-element.76, pred[40,4]{0,1:T(4,128)(4,1)S(1)} %get-tuple-element.74, f32[4,8,256,256]{3,1,2,0:T(8,128)} %copy.82), kind=kOutput, calls=%fused_computation.9 | convolution fusion | flops 1006635520 | bytes 18874888 | tf_op jit(solution)/shard_map/dot_general | solution.py:19
  371.5 11.5 %copy.54 = f32[40,256,256]{1,2,0:T(8,128)} copy(f32[40,256,256]{2,0,1:T(8,128)} %fusion.3) | data formatting | bytes 20971520 | tf_op jit(solution)/shard_map/dot_general | solution.py:19
  382.9 7.6 maximum_subtract_fusion
  390.6 4.1 copy-done
  395.6 1.3 slice_bitcast_fusion
  397.5 80.8 %all-reduce.14.cloned.1.call-done = f32[256,256]{0,1:T(8,128)} async-done(((f32[256,256]{0,1:T(8,128)}), f32[256,256]{0,1:T(8,128)}) %all-reduce.14.cloned.1.call-update) | async-done | bytes 262160 | tf_op jit(solution)/shard_map/psum | solution.py:14
  478.5 11.7 %cholesky.164 = f32[128,128]{1,0:T(8,128)S(1)} custom-call(f32[128,128]{1,0:T(8,128)S(1)} %cholesky.197), custom_call_target="Cholesky" | custom-call | tf_op jit(solution)/shard_map/jit(cholesky)/cholesky | solution.py:35
  491.0 9.8 %custom-call.15 = f32[1,128,128]{1,2,0:T(8,128)S(1)} custom-call(f32[1,128,128]{2,1,0:T(8,128)S(1)} %get-tuple-element.62), custom_call_target="InvertDiagBlocksLowerTriangular" | custom-call | tf_op jit(solution)/shard_map/jit(cholesky)/cholesky | solution.py:35
  501.3 11.7 %cholesky.181 = f32[128,128]{1,0:T(8,128)S(1)} custom-call(f32[128,128]{1,0:T(8,128)S(1)} %convolution_subtract_fusion.2), custom_call_target="Cholesky" | custom-call | tf_op jit(solution)/shard_map/jit(cholesky)/cholesky | solution.py:35
  515.3 4.4 while.5
  516.2 1.4 bitcast_dynamic-update-slice_fusion.5
  518.3 1.4 bitcast_dynamic-update-slice_fusion.5
  519.7 19.7 %custom-call.16 = f32[2,128,128]{1,2,0:T(8,128)S(1)} custom-call(f32[2,128,128]{2,1,0:T(8,128)S(1)} %get-tuple-element.22), custom_call_target="InvertDiagBlocksLowerTriangular" | custom-call | tf_op jit(solution)/shard_map/triangular_solve/custom-call.0 | solution.py:38
  542.0 2.5 broadcast_select_fusion
  544.6 59.6 %all-reduce.16.cloned.1.call-done = f32[4,256,256]{1,2,0:T(8,128)} async-done(((f32[4,256,256]{1,2,0:T(8,128)}), f32[4,256,256]{1,2,0:T(8,128)}) %all-reduce.16.cloned.1.call-update) | async-done | bytes 1048592 | tf_op jit(solution)/shard_map/psum | solution.py:14
  604.1 2.5 copy.61
  606.7 8.4 %slice.131 = f32[36,256,256]{1,2,0:T(8,128)} slice(f32[40,256,256]{1,2,0:T(8,128)} %copy-done), slice={[4:40], [0:256], [0:256]} | slice | bytes 18874368 | tf_op jit(solution)/shard_map/slice | solution.py:43
  615.1 105.9 %all-gather.5.cloned.1.call-done = f32[64,256,256]{2,1,0:T(8,128)} async-done(((f32[4,256,256]{2,1,0:T(8,128)}), f32[64,256,256]{2,1,0:T(8,128)}) %all-gather.5.cloned.1.call-update) | async-done | bytes 16777232 | tf_op jit(solution)/shard_map/all_gather | solution.py:50
  721.0 1.7 constant_dynamic-slice_fusion.3
  722.7 9.3 %convolution_bitcast_fusion = f32[4,8,256,256]{2,3,0,1:T(8,128)} fusion(f32[4,256,256]{2,1,0:T(8,128)S(1)} %get-tuple-element.56, f32[4,256,256]{2,1,0:T(8,128)S(1)} %get-tuple-element.55, f32[4,256,256]{1,2,0:T(8,128)S(1)} %copy-done.2), kind=kOutput, calls=%fused_computation.12 | convolution fusion | flops 6442975232 | bytes 11534336 | tf_op jit(solution)/shard_map/iab,jcb->ijac/dot_general | solution.py:60
  732.0 10.4 %copy.83 = f32[4,8,256,256]{3,1,2,0:T(8,128)} copy(f32[4,8,256,256]{2,3,0,1:T(8,128)} %convolution_bitcast_fusion) | data formatting | bytes 16777216
  742.5 9.4 %fusion = f32[40,256,256]{2,0,1:T(8,128)} fusion(pred[40]{0:T(512)(128)(4,1)S(1)} %get-tuple-element.67, pred[40,8]{0,1:T(8,128)(4,1)S(1)} %get-tuple-element.75, pred[40,4]{0,1:T(4,128)(4,1)S(1)} %get-tuple-element.73, f32[4,8,256,256]{3,1,2,0:T(8,128)} %copy.83), kind=kOutput, calls=%fused_computation.6 | convolution fusion | flops 1006635520 | bytes 18874888 | tf_op jit(solution)/shard_map/dot_general | solution.py:19
  751.9 11.5 %copy.65 = f32[40,256,256]{1,2,0:T(8,128)} copy(f32[40,256,256]{2,0,1:T(8,128)} %fusion) | data formatting | bytes 20971520 | tf_op jit(solution)/shard_map/dot_general | solution.py:19
  763.3 11.4 %maximum_subtract_fusion.1 = f32[40,256,256]{1,2,0:T(8,128)} fusion(f32[40,256,256]{1,2,0:T(8,128)} %copy.65, f32[36,256,256]{1,2,0:T(8,128)} %slice.131, f32[4,256,256]{1,2,0:T(8,128)S(1)} %get-tuple-element.44), kind=kLoop, calls=%fused_computation.5 | loop fusion | flops 5242880 | bytes 31457280 | tf_op jit(solution)/shard_map/sub | solution.py:22
  774.8 11.4 %copy.66 = f32[40,256,256]{2,1,0:T(8,128)} copy(f32[40,256,256]{1,2,0:T(8,128)} %maximum_subtract_fusion.1) | data formatting | bytes 20971520 | tf_op jit(solution)/shard_map/sub | solution.py:22
  (91 shorter events, 18.1 us)
Async XLA Ops:
  6.5 89.5 %all-reduce.10.cloned.1.call-start = ((), (), s32[]{:S(2)}) async-start(), calls=%async_computation | async-start | bytes 524288 | tf_op jit(solution)/shard_map/psum | solution.py:14
  8.4 215.5 %all-reduce.12.cloned.1.call-start = ((), (), s32[]{:S(2)}) async-start(), calls=%async_computation.1 | async-start | bytes 2097152 | tf_op jit(solution)/shard_map/psum | solution.py:14
  138.5 88.0 %copy-start.3 = (s32[40,2]{0,1:T(2,128)S(1)}, s32[40,2]{0,1:T(2,128)}, u32[]{:S(2)}) copy-start(s32[40,2]{0,1:T(2,128)} %param.6) | copy-start | bytes 964
  164.3 176.5 %all-gather.3.cloned.1.call-start = ((), (), s32[]{:S(2)}) async-start(), calls=%async_computation.2 | async-start | bytes 17825792 | tf_op jit(solution)/shard_map/all_gather | solution.py:50
  226.5 251.8 %all-reduce.14.cloned.1.call-start = ((), (), s32[]{:S(2)}) async-start(), calls=%async_computation.3 | async-start | bytes 524288 | tf_op jit(solution)/shard_map/psum | solution.py:14
  242.2 9.8 %copy-start.4 = (u32[128]{0:T(128)S(1)}, u32[128]{0:T(128)}, u32[]{:S(2)}) copy-start(u32[128]{0:T(128)} %constant.104) | copy-start | bytes 1540
  242.2 100.4 %copy-start.1 = (f32[4,256,256]{1,2,0:T(8,128)S(1)}, f32[4,256,256]{1,2,0:T(8,128)}, u32[]{:S(2)}) copy-start(f32[4,256,256]{1,2,0:T(8,128)} %all-reduce.12.cloned.1.call-done) | copy-start | bytes 3145732
  390.5 4.1 copy-start
  395.4 208.7 %all-reduce.16.cloned.1.call-start = ((), (), s32[]{:S(2)}) async-start(), calls=%async_computation.4 | async-start | bytes 2097152 | tf_op jit(solution)/shard_map/psum | solution.py:14
  544.5 176.5 %all-gather.5.cloned.1.call-start = ((), (), s32[]{:S(2)}) async-start(), calls=%async_computation.5 | async-start | bytes 17825792 | tf_op jit(solution)/shard_map/all_gather | solution.py:50
  606.7 116.0 %copy-start.2 = (f32[4,256,256]{1,2,0:T(8,128)S(1)}, f32[4,256,256]{1,2,0:T(8,128)}, u32[]{:S(2)}) copy-start(f32[4,256,256]{1,2,0:T(8,128)} %all-reduce.16.cloned.1.call-done) | copy-start | bytes 3145732
Sparse Core Ops, SparseCore 0:
  10.5 85.4 all-reduce.9
  164.5 59.3 all-reduce.11
  226.6 114.2 all-gather.2
  395.5 82.7 all-reduce.13
  544.6 59.4 all-reduce.15
  606.8 114.1 all-gather.4
where the time goes:
time: 804 us; the launch traced here: 793 us
  waiting for transfers between devices  464 us (58%)
  other arithmetic  134 us (17%)
  local copies, waits for them, and re-layouts  114 us (14%)
  matrix products  41.8 us (5%)
  blocking collectives  20 us (2%)
  between operations  17.7 us (2%)
    psum x4, waiting for transfers between devices, broadcast(): return lax.psum(jnp.where(mine, x, jnp.zeros_like(x)), axis)  285 us
    all_gather x2, waiting for transfers between devices, factor_step(): lax.all_gather(row_blocks, 'narrow', axis=0, tiled=True)  179 us
    another operation x13, other arithmetic, factor_step(): lower_factor = jnp.linalg.cholesky(pivot_block)  68.7 us
    another operation x7, other arithmetic, factor_step(): lax.linalg.triangular_solve(lower_factor, stacked, left_side=True, lower=...  40.3 us
    unnamed x22, local copies, waits for them, and re-layouts  36.6 us
    dot_general x2, local copies, waits for them, and re-layouts, subtract_terms(): jnp.dot(selector, flat_products, precision=HIGHEST_PRECISION, preferred_e...  23 us
    sub x2, other arithmetic, subtract_terms(): return current - removed.reshape(current.shape)  19 us
    dot_general x2, matrix products, subtract_terms(): jnp.dot(selector, flat_products, precision=HIGHEST_PRECISION, preferred_e...  18.8 us
  transfers between devices with their start and end apart: 6, of which 6 were waited for; matrix products, arithmetic and copies ran while one was open for 4% of the time, Pallas kernels for 0%

commit v1 on v0

v1 whole, which is shorter than its diff:
```python
import jax
import jax.numpy as jnp
from jax import lax
from jax.experimental import pallas as pl
from jax.experimental.pallas import tpu as pltpu
from jax.sharding import PartitionSpec as P

PR = 4
W = 256
H = 128
G = 8
CHUNKS = 16
RING = 4
ROWS = 16
CHILDREN = (85, 40969, 4097, 32857)
MESH = pl.DeviceIdType.MESH
HIGHEST = lax.Precision.HIGHEST
F32 = jnp.float32


def dot_nn(a, b):
    return lax.dot_general(a, b, (((1,), (0,)), ((), ())), precision=HIGHEST, preferred_element_type=F32)


def dot_nt(a, b):
    return lax.dot_general(a, b, (((1,), (1,)), ((), ())), precision=HIGHEST, preferred_element_type=F32)


def tree_sum(terms):
    terms = list(terms)
    while len(terms) > 1:
        terms = [terms[i] + terms[i + 1] if i + 1 < len(terms) else terms[i] for i in range(0, len(terms), 2)]
    return terms[0]


def eliminate(p, c_ref, u_ref, x_ref):
    lo = p * G
    lane = lax.broadcasted_iota(jnp.int32, (G, H), 1)
    sub = lax.broadcasted_iota(jnp.int32, (G, H), 0)
    rows = c_ref[lo : lo + G, :]
    cols = [jnp.broadcast_to(rows[:, lo + j : lo + j + 1], (G, H)) for j in range(G)]
    a = {(i, j): jnp.broadcast_to(cols[j][i : i + 1, :], (G, H)) for j in range(G) for i in range(j, G)}
    low, inv, x = {}, [None] * G, {}
    for j in range(G):
        inv[j] = lax.rsqrt(a[j, j])
        for i in range(j + 1, G):
            low[i, j] = a[i, j] * inv[j]
        for k in range(j + 1, G):
            for i in range(k, G):
                a[i, k] = a[i, k] - low[i, j] * low[k, j]
    for j in range(G):
        x[j, j] = inv[j]
        for i in range(j + 1, G):
            x[i, j] = -(inv[i] * tree_sum([low[i, k] * x[k, j] for k in range(j, i)]))
    in_block = (lane >= lo) & (lane < lo + G)
    rows_with_eye = jnp.where(in_block, (lane - lo == sub).astype(F32), rows)

    def column(entry, ids):
        out = jnp.zeros((G, H), F32)
        for i in ids:
            out = jnp.where(sub == i, entry(i), out)
        return out

    def row(v, k):
        return jnp.broadcast_to(v[k : k + 1, :], (G, H))

    weights = [column(lambda i: x[i, k], range(k, G)) for k in range(G)]
    weights_t = [column(lambda i: x[k, i], range(0, k + 1)) for k in range(G)]
    reduced = tree_sum([weights[k] * row(rows_with_eye, k) for k in range(G)])
    upper = tree_sum([weights[k] * row(rows, k) for k in range(G)])
    u_ref[lo : lo + G, :] = jnp.where(lane >= lo + sub, upper, 0.0)
    x_ref[lo : lo + G, :] = jnp.where(lane < lo + G, reduced, 0.0)
    solved = tree_sum([weights_t[k] * row(reduced, k) for k in range(G)])
    solved_rows = [row(solved, k) for k in range(G)]
    for m in range(p + 1, H // G):
        old = c_ref[m * G : (m + 1) * G, :]
        taken = [jnp.broadcast_to(old[:, lo + k : lo + k + 1], (G, H)) * solved_rows[k] for k in range(G)]
        c_ref[m * G : (m + 1) * G, :] = jnp.where(in_block, 0.0, old) - tree_sum(taken)


def factor_128(c_ref, u_ref, x_ref):
    for p in range(H // G):
        eliminate(p, c_ref, u_ref, x_ref)


def factor_256(src, low_ref, inv_ref, c_ref, u_ref, x_ref, g_ref):
    zero = jnp.zeros((H, H), F32)
    c_ref[...] = src[0:H, 0:H]
    factor_128(c_ref, u_ref, x_ref)
    x1 = x_ref[...]
    inv_ref[0:H, 0:H] = x1
    inv_ref[0:H, H:W] = zero
    low_ref[0:H, 0:H] = u_ref[...].T
    low_ref[0:H, H:W] = zero
    below = dot_nt(src[H:W, 0:H], x1)
    low_ref[H:W, 0:H] = below
    c_ref[...] = src[H:W, H:W] - dot_nt(below, below)
    g_ref[...] = dot_nn(below, x1)
    factor_128(c_ref, u_ref, x_ref)
    x2 = x_ref[...]
    inv_ref[H:W, H:W] = x2
    low_ref[H:W, H:W] = u_ref[...].T
    inv_ref[H:W, 0:H] = -dot_nn(x2, g_ref[...])


def send_kernel(
    blk, idt, buf, idb, ch,
    dsrc, dpiece, dfull, chv, c_ref, u_ref, x_ref, g_ref,
    rs, ps, ri, pi, s_src, s_piece, s_full, s_to0, s_ch,
    t_x, t_tree, t_ix, t_itree, t_to0, t_ito0, t_src, t_scat, t_dx, t_gath, t_first, t_ch,
):
    w = lax.axis_index("wide")
    n = lax.axis_index("narrow")
    x, core = w // 2, w % 2
    y, z = n // RING, n % RING
    partner = (x * 2 + 1 - core, n)
    barrier = pltpu.get_barrier_semaphore()

    def chunk(ref, slot, k):
        return ref.at[slot, k // 2, pl.ds(pl.multiple_of((k % 2) * H, H), H)]

    def remote(src, dst, send, recv, device):
        return pltpu.make_async_remote_copy(
            src_ref=src, dst_ref=dst, send_sem=send, recv_sem=recv, device_id=device, device_id_type=MESH
        )

    def wait_bytes(ref, sem):
        pltpu.make_async_copy(ref, ref, sem).wait()

    def signal(device):
        pl.semaphore_signal(barrier, inc=1, device_id=device, device_id_type=MESH)

    def at_x(dx):
        return (lax.rem(x + dx, RING) * 2 + 1, n)

    @pl.when(core == 0)
    def _():
        @pl.loop(0, RING * RING)
        def _(i):
            signal((x * 2 + 1, i))

        pl.semaphore_wait(barrier, 1)

        @pl.when(x == 0)
        def _():
            @pl.when(n < 2)
            def _():
                remote(blk.at[0], dsrc, t_src, s_src, partner).start()

            remote(idt, idb.at[4, 0], t_first.at[0], ri, partner).start()
            for k in range(CHUNKS // 2):
                remote(chunk_of_block(blk, k), chunk(buf, 4, k), t_first.at[1], rs.at[k], partner).start()

        wait_bytes(dfull.at[0], s_full.at[0])
        factor_256(dfull.at[0], chv.at[0], chv.at[1], c_ref, u_ref, x_ref, g_ref)
        wait_bytes(dfull.at[1], s_full.at[1])
        l10 = dot_nt(dfull[1], chv[1])
        chv[2] = l10
        wait_bytes(dfull.at[2], s_full.at[2])
        dfull[2] = dfull[2] - dot_nt(l10, l10)
        factor_256(dfull.at[2], chv.at[3], chv.at[4], c_ref, u_ref, x_ref, g_ref)
        remote(chv, ch, t_ch.at[0], s_ch, partner).start()
        own = pltpu.make_async_copy(chv, ch, t_ch.at[1])
        own.start()

        @pl.when(x == 0)
        def _():
            @pl.when(n < 2)
            def _():
                wait_bytes(dsrc, t_src)

            wait_bytes(idt, t_first.at[0])
            wait_bytes(buf.at[4, pl.ds(0, PR)], t_first.at[1])

        for h in range(2):
            @pl.when(n != 2 * x + 8 * h)
            def _():
                wait_bytes(idb.at[2 * h], s_to0.at[2 * h])
                wait_bytes(buf.at[2 * h], s_to0.at[2 * h + 1])

        wait_bytes(idb.at[4], s_to0.at[4])
        wait_bytes(buf.at[4], s_to0.at[5])
        wait_bytes(chv, t_ch.at[0])
        own.wait()

    @pl.when(core == 1)
    def _():
        signal(partner)
        for dx in range(1, RING):
            signal(at_x(dx))

        @pl.loop(0, RING * RING)
        def _(i):
            @pl.when(i != n)
            def _():
                signal((w, i))

        pl.semaphore_wait(barrier, 2 * RING * RING - 1 + RING - 1)

        def scatter(b, src):
            @pl.loop(0, RING * RING)
            def _(i):
                part = src.at[pl.ds(pl.multiple_of(i * ROWS, ROWS), ROWS)]

                @pl.when(i != n)
                def _():
                    remote(part, dpiece.at[b], t_scat.at[b], s_piece.at[b], (w, i)).start()

                @pl.when(i == n)
                def _():
                    pltpu.make_async_copy(part, dpiece.at[b], s_piece.at[b]).start()

        @pl.when(x == 0)
        def _():
            @pl.when(n == 1)
            def _():
                scatter(2, blk.at[0])

            @pl.when(n < 2)
            def _():
                wait_bytes(dsrc, s_src)

                @pl.when(n == 0)
                def _():
                    scatter(0, dsrc)

                @pl.when(n == 1)
                def _():
                    scatter(1, dsrc)

            pltpu.make_async_copy(idt, idb.at[4, 1], ri).start()
            for k in range(CHUNKS // 2, CHUNKS):
                pltpu.make_async_copy(chunk_of_block(blk, k - CHUNKS // 2), chunk(buf, 4, k), rs.at[k]).start()
            wait_bytes(idb.at[4], ri)
            for j, dx in enumerate((1, RING - 1)):
                remote(idb.at[4], idb.at[4], t_ix.at[j], ri, at_x(dx)).start()

            @pl.loop(0, CHUNKS)
            def _(k):
                wait_bytes(chunk(buf, 4, k), rs.at[k])
                for j, dx in enumerate((1, RING - 1)):
                    remote(chunk(buf, 4, k), chunk(buf, 4, k), t_x.at[j], rs.at[k], at_x(dx)).start()

        for b in range(3):
            wait_bytes(dpiece.at[b], s_piece.at[b])

            @pl.when(x == 0)
            def _():
                for dx in range(1, RING):
                    remote(dpiece.at[b], dpiece.at[b], t_dx.at[b], s_piece.at[b], at_x(dx)).start()

            mine = pl.ds(pl.multiple_of(n * ROWS, ROWS), ROWS)

            @pl.loop(0, RING * RING)
            def _(i):
                remote(dpiece.at[b], dfull.at[b, mine], t_gath.at[b], s_full.at[b], (x * 2, i)).start()

        y_rel = lax.rem(y - x // 2 + RING, RING)
        z_rel = lax.rem(z - 2 * (x % 2) + RING, RING)
        steps = ((1, 0), (RING - 1, 0), (0, 1), (0, RING - 1))
        near = [(w, lax.rem(y + dy, RING) * RING + lax.rem(z + dz, RING)) for dy, dz in steps]
        sources, sends = [], []
        for g in range(4):
            h, q = g // 2, g % 2
            y_own = lax.rem(y_rel + 2 * h, RING)
            z_own = z_rel if q == 0 else lax.rem(1 - z_rel + RING, RING)
            index = y_own * RING + z_own
            flags = [(jnp.int32(mask) >> index) & 1 for mask in CHILDREN]
            if q == 1:
                flags[2], flags[3] = flags[3], flags[2]
            sources.append(index == 0)
            sends.append(flags)

        def pass_on(part, row_recv, row_from_x, tree_recv, x_send, tree_send, to0, to0_send, to0_row, x_odd):
            @pl.when(x != 0)
            def _():
                wait_bytes(part(4), row_recv)

                @pl.when(x == 1 + 2 * x_odd)
                def _():
                    remote(part(4), part(4), x_send, row_recv, (5, n)).start()

            remote(part(4), part(4), to0_send(4), to0_row, partner).start()
            for g in range(4):
                @pl.when(sources[g])
                def _():
                    for d in range(4):
                        remote(part(4), part(g), tree_send(g, d), tree_recv(g), near[d]).start()

                @pl.when(jnp.logical_not(sources[g]))
                def _():
                    wait_bytes(part(g), tree_recv(g))
                    for d in range(4):
                        @pl.when(sends[g][d] == 1)
                        def _():
                            remote(part(g), part(g), tree_send(g, d), tree_recv(g), near[d]).start()

                    if g % 2 == 0:
                        remote(part(g), part(g), to0_send(g), to0(g), partner).start()

        pass_on(
            lambda g: idb.at[g], ri, None, lambda g: pi.at[g], t_ix.at[0], lambda g, d: t_itree.at[g, d],
            lambda g: s_to0.at[g], lambda g: t_ito0.at[g], s_to0.at[4], 0,
        )

        @pl.loop(0, CHUNKS)
        def _(k):
            pass_on(
                lambda g: chunk(buf, g, k), rs.at[k], None, lambda g: ps.at[g, k], t_x.at[0],
                lambda g, d: t_tree.at[g, d], lambda g: s_to0.at[g + 1], lambda g: t_to0.at[g], s_to0.at[5], k % 2,
            )

        @pl.when(x == 0)
        def _():
            for j in range(2):
                wait_bytes(idb.at[4], t_ix.at[j])
                wait_bytes(buf.at[4], t_x.at[j])
            for b in range(3):
                for dx in range(1, RING):
                    wait_bytes(dpiece.at[b], t_dx.at[b])

            @pl.when(n == 0)
            def _():
                wait_bytes(dfull.at[0, pl.ds(0, W - ROWS)], t_scat.at[0])

            @pl.when(n == 1)
            def _():
                for b in (1, 2):
                    wait_bytes(dfull.at[b, pl.ds(0, W - ROWS)], t_scat.at[b])

        @pl.when(x == 1)
        def _():
            wait_bytes(idb.at[4], t_ix.at[0])

        @pl.when(x % 2 == 1)
        def _():
            wait_bytes(buf.at[4, pl.ds(0, PR)], t_x.at[0])

        for b in range(3):
            wait_bytes(dfull.at[b], t_gath.at[b])
        for g in range(4):
            for d in range(4):
                @pl.when(sources[g] | (sends[g][d] == 1))
                def _():
                    wait_bytes(idb.at[g], t_itree.at[g, d])
                    wait_bytes(buf.at[g], t_tree.at[g, d])
            if g % 2 == 0:
                @pl.when(jnp.logical_not(sources[g]))
                def _():
                    wait_bytes(idb.at[g], t_ito0.at[g])
                    wait_bytes(buf.at[g], t_to0.at[g])
        wait_bytes(idb.at[4], t_ito0.at[4])
        wait_bytes(buf.at[4], t_to0.at[4])
        wait_bytes(ch, s_ch)


def chunk_of_block(blk, k):
    return blk.at[k // 2, pl.ds((k % 2) * H, H)]


def split(a):
    high = a.astype(jnp.bfloat16)
    return high, (a - high.astype(F32)).astype(jnp.bfloat16)


def local_kernel(
    bmap, idb, blk, buf, ch, out,
    vb, pan, chv, low_r, low_c, row3, col3, g_ref, s_in, s_out, s_pan, s_ch,
):
    w = lax.axis_index("wide")
    n = lax.axis_index("narrow")
    x, core = w // 2, w % 2
    slots = blk.shape[0]
    piece = [jnp.where(n == w + 8 * h, 4, 2 * h + core) for h in range(2)]
    copies = [
        pltpu.make_async_copy(ch, chv, s_ch),
        pltpu.make_async_copy(buf.at[4], pan.at[0], s_pan.at[0]),
        pltpu.make_async_copy(buf.at[piece[0]], pan.at[1], s_pan.at[1]),
        pltpu.make_async_copy(buf.at[piece[1]], pan.at[2], s_pan.at[2]),
    ]
    for copy in copies:
        copy.start()

    @pl.loop(0, slots)
    def _(s):
        pltpu.make_async_copy(blk.at[s], vb.at[s], s_in.at[s]).start()

    for copy in copies:
        copy.wait()

    def find(slot, column, block_row):
        found = jnp.int32(-1)
        for i in range(PR):
            found = jnp.where(idb[slot, column, i, 0] == block_row, i, found)
        return found

    def store_row(i, value):
        low_r[i] = value
        high, rest = split(value)
        row3[i, :, 0:W] = high
        row3[i, :, W : 2 * W] = high
        row3[i, :, 2 * W : 3 * W] = rest

    def store_col(j, value):
        high, rest = split(value)
        col3[j, 0:W, :] = high
        col3[j, W : 2 * W, :] = rest
        col3[j, 2 * W : 3 * W, :] = high

    @pl.loop(0, PR)
    def _(i):
        store_row(i, dot_nt(pan[0, i], chv[1]))

    @pl.loop(0, 2 * PR)
    def _(j):
        value = dot_nt(chv[1], pan[1 + j // PR, j % PR])
        low_c[j] = value
        store_col(j, value)

    g_ref[...] = dot_nn(chv[4], chv[2])

    @pl.loop(0, PR)
    def _(i):
        from_first = find(4, 0, idb[4, 1, i, 0])
        pan[0, i] = dot_nt(pan[0, PR + i], chv[4])

        @pl.when((from_first >= 0) & (idb[4, 1, i, 0] > 0))
        def _():
            pan[0, i] = pan[0, i] - dot_nt(low_r[jnp.maximum(from_first, 0)], g_ref[...])

        store_row(PR + i, pan[0, i])

    @pl.loop(0, 2 * PR)
    def _(j):
        h, i = j // PR, j % PR
        slot = jnp.where(h == 0, piece[0], piece[1])
        block_row = idb[slot, 1, i, 0]
        from_first = find(slot, 0, block_row)
        pan[1 + h, i] = dot_nt(chv[4], pan[1 + h, PR + i])

        @pl.when((from_first >= 0) & (block_row > 0))
        def _():
            pan[1 + h, i] = pan[1 + h, i] - dot_nn(g_ref[...], low_c[h * PR + jnp.maximum(from_first, 0)])

        store_col(2 * PR + j, pan[1 + h, i])

    @pl.loop(0, slots)
    def _(s):
        r, c = bmap[s, 0], bmap[s, 1]
        h = (c % 16) // 8
        slot = jnp.where(h == 0, piece[0], piece[1])
        pltpu.make_async_copy(blk.at[s], vb.at[s], s_in.at[s]).wait()
        for column in range(2):
            i, j = find(4, column, r), find(slot, column, c)

            @pl.when((r > column) & (c > column) & (i >= 0) & (j >= 0))
            def _():
                vb[s] = vb[s] - jnp.dot(
                    row3[column * PR + jnp.maximum(i, 0)],
                    col3[column * 2 * PR + h * PR + jnp.maximum(j, 0)],
                    preferred_element_type=F32,
                )

            @pl.when((c == column) & (i >= 0))
            def _():
                vb[s] = low_r[column * PR + jnp.maximum(i, 0)]

                @pl.when(r == column)
                def _():
                    vb[s] = chv[3 * column]

        pltpu.make_async_copy(vb.at[s], out.at[s], s_out).start()

    pltpu.make_async_copy(vb, out, s_out).wait()


def on_device(blocks, block_map):
    ids = jnp.broadcast_to(jnp.pad(block_map[:PR, 0], (0, G - PR))[:, None], (G, H))
    anywhere = pl.BlockSpec(memory_space=pl.ANY)
    dma = pltpu.SemaphoreType.DMA
    vmem = pltpu.VMEM
    buf, idb, ch = pl.pallas_call(
        send_kernel,
        out_shape=[
            jax.ShapeDtypeStruct((5, 2 * PR, W, W), F32),
            jax.ShapeDtypeStruct((5, 2, G, H), jnp.int32),
            jax.ShapeDtypeStruct((5, W, W), F32),
        ],
        in_specs=[anywhere, anywhere],
        out_specs=[anywhere, anywhere, anywhere],
        scratch_shapes=[
            vmem((W, W), F32), vmem((3, ROWS, W), F32), vmem((3, W, W), F32), vmem((5, W, W), F32),
            vmem((H, H), F32), vmem((H, H), F32), vmem((H, H), F32), vmem((H, H), F32),
            dma((CHUNKS,)), dma((4, CHUNKS)), dma, dma((4,)), dma, dma((3,)), dma((3,)), dma((6,)), dma,
            dma((2,)), dma((4, 4)), dma((2,)), dma((4, 4)), dma((5,)), dma((5,)), dma, dma((3,)), dma((3,)), dma((3,)),
            dma((2,)), dma((2,)),
        ],
        compiler_params=pltpu.CompilerParams(collective_id=0, has_side_effects=True, vmem_limit_bytes=16 * 2**20),
    )(blocks, ids)
    slots = blocks.shape[0]
    return pl.pallas_call(
        local_kernel,
        out_shape=jax.ShapeDtypeStruct(blocks.shape, F32),
        in_specs=[
            pl.BlockSpec(memory_space=pltpu.SMEM), pl.BlockSpec(memory_space=pltpu.SMEM), anywhere, anywhere, anywhere,
        ],
        out_specs=anywhere,
        scratch_shapes=[
            vmem((slots, W, W), F32), vmem((3, 2 * PR, W, W), F32), vmem((5, W, W), F32),
            vmem((2 * PR, W, W), F32), vmem((2 * PR, W, W), F32),
            vmem((2 * PR, W, 3 * W), jnp.bfloat16), vmem((4 * PR, 3 * W, W), jnp.bfloat16), vmem((W, W), F32),
            dma((slots,)), dma, dma((3,)), dma,
        ],
        compiler_params=pltpu.CompilerParams(vmem_limit_bytes=44 * 2**20),
    )(block_map, idb, blocks, buf, ch)


def solution(mesh):
    return jax.shard_map(
        on_device,
        mesh=mesh,
        in_specs=(P(("wide", "narrow"), None, None), P(("wide", "narrow"), None)),
        out_specs=P(("wide", "narrow"), None, None),
        check_vma=False,
    )
```

time: 804 us -> 536 us (0.67); the launches traced: 793 us -> 536 us
  Pallas kernels: 0 us -> 526 us
  waiting for transfers between devices: 464 us -> 0 us
  other arithmetic: 134 us -> 0 us
  local copies, waits for them, and re-layouts: 114 us -> 9.48 us
  matrix products: 41.8 us -> 0 us
  blocking collectives: 20 us -> 0 us
  between operations: 17.7 us -> 0.2 us
    pallas_call x0 -> x2, Pallas kernels: none -> 526 us  [the longest x1 493 us: on_device(): pl.pallas_call(send_kernel, out_shape=[jax.ShapeDtypeStruct((5, 2 * PR, W...]
    psum x4 -> x0, waiting for transfers between devices: 285 us -> none  [broadcast(): return lax.psum(jnp.where(mine, x, jnp.zeros_like(x)), axis)]
    all_gather x2 -> x0, waiting for transfers between devices: 179 us -> none  [factor_step(): lax.all_gather(row_blocks, 'narrow', axis=0, tiled=True)]
    another operation x20 -> x0, other arithmetic: 109 us -> none  [the longest x13 68.7 us: factor_step(): lower_factor = jnp.linalg.cholesky(pivot_block)]
    dot_general x4 -> x0, matrix products: 37.2 us -> none  [the longest x2 18.8 us: subtract_terms(): jnp.dot(selector, flat_products, precision=HIGHEST_PRECISION, preferred_e...]
    unnamed x22 -> x5, local copies, waits for them, and re-layouts: 36.6 us -> 8.72 us
    dot_general x2 -> x0, local copies, waits for them, and re-layouts: 23 us -> none  [subtract_terms(): jnp.dot(selector, flat_products, precision=HIGHEST_PRECISION, preferred_e...]
    slice x5 -> x0, local copies, waits for them, and re-layouts: 19.6 us -> none  [the longest x2 17.3 us: factor_step(): blocks = jnp.concatenate([panel_new, blocks[PR_DEV:]], axis=0)]
  transfers between devices with their start and end apart: 6 -> 0, of which waited for: 6 -> 0; matrix products, arithmetic and copies ran while one was open for 4% -> 0% of each run, Pallas kernels for 0% -> 0%
where the time goes in v1:
time: 536 us
  Pallas kernels  526 us (98%)
  local copies, waits for them, and re-layouts  9.48 us (2%)
    pallas_call x1, Pallas kernels, on_device(): pl.pallas_call(send_kernel, out_shape=[jax.ShapeDtypeStruct((5, 2 * PR, W...  493 us
    pallas_call x1, Pallas kernels, on_device(): pl.pallas_call(local_kernel, out_shape=jax.ShapeDtypeStruct(blocks.shape,...  33.7 us

profile of v1, /device:TPU:5, one launch (start us, length us, event | category | flops | bytes accessed | tf_op | source)
XLA Modules:
  0.0 536.1 jit_solution(12637260830037744162)
XLA Ops:
  0.0 0.7 slice_bitcast_fusion
  0.7 0.1 broadcast_in_dim.2.idt
  0.8 0.8 copy.3.bmap
  1.5 0.0 copy-start
  1.5 4.0 copy-done
  5.5 492.7 %shard_map.28 = (f32[5,8,256,256]{3,2,1,0:T(8,128)S(1)}, s32[5,2,8,128]{3,2,1,0:T(8,128)S(1)}, f32[5,256,256]{2,1,0:T(8,128)S(1)}) custom-call(f32[40,256,256]{2,1,0:T(8,128)S(1)} %copy-done, s32[8,128]{1,0:T(8,128)S(1)} %broadcast_in_dim.2.idt), custom_call_target="tpu_custom_call" | custom-call | tf_op jit(solution)/shard_map/pallas_call | solution.py:482
  498.2 0.0 copy-start.1
  498.2 4.0 copy-done.1
  502.2 33.7 %shard_map.29 = f32[40,256,256]{2,1,0:T(8,128)} custom-call(s32[40,2]{1,0:T(8,128)S(1)} %copy.3.bmap, s32[5,2,8,128]{3,2,1,0:T(8,128)S(1)} %get-tuple-element.8.idb, f32[40,256,256]{2,1,0:T(8,128)} %blk.3, f32[5,8,256,256]{3,2,1,0:T(8,128)} %copy-done.1, f32[5,256,256]{2,1,0:T(8,128)S(1)} %get-tuple-element.10.ch), custom_call_target="tpu_custom_call" | custom-call | tf_op jit(solution)/shard_map/pallas_call | solution.py:501
  (1 shorter events, 0.0 us)
Async XLA Ops:
  1.5 4.0 copy-start
  498.2 4.0 copy-start.1

commit v2 on v1

--- a/solution.py
+++ b/solution.py
@@ -9,10 +9,14 @@
 W = 256
 H = 128
 G = 8
-CHUNKS = 16
+CHUNKS = 32
+PARTS = CHUNKS // (2 * PR)
+PART = W // PARTS
 RING = 4
 ROWS = 16
 CHILDREN = (85, 40969, 4097, 32857)
+DEPTH = (23130, 60356, 1056)
+SKEW = 4
 MESH = pl.DeviceIdType.MESH
 HIGHEST = lax.Precision.HIGHEST
 F32 = jnp.float32
@@ -105,7 +109,7 @@
 
 def send_kernel(
     blk, idt, buf, idb, ch,
-    dsrc, dpiece, dfull, chv, c_ref, u_ref, x_ref, g_ref,
+    dsrc, dpiece, held, dfull, chv, c_ref, u_ref, x_ref, g_ref,
     rs, ps, ri, pi, s_src, s_piece, s_full, s_to0, s_ch,
     t_x, t_tree, t_ix, t_itree, t_to0, t_ito0, t_src, t_scat, t_dx, t_gath, t_first, t_ch,
 ):
@@ -117,7 +121,7 @@
     barrier = pltpu.get_barrier_semaphore()
 
     def chunk(ref, slot, k):
-        return ref.at[slot, k // 2, pl.ds(pl.multiple_of((k % 2) * H, H), H)]
+        return ref.at[slot, k // PARTS, pl.ds(pl.multiple_of((k % PARTS) * PART, PART), PART)]
 
     def remote(src, dst, send, recv, device):
         return pltpu.make_async_remote_copy(
@@ -229,17 +233,10 @@
                     scatter(1, dsrc)
 
             pltpu.make_async_copy(idt, idb.at[4, 1], ri).start()
+            pltpu.make_async_copy(blk.at[pl.ds(0, PR)], held, t_first.at[0]).start()
+            wait_bytes(held, t_first.at[0])
             for k in range(CHUNKS // 2, CHUNKS):
-                pltpu.make_async_copy(chunk_of_block(blk, k - CHUNKS // 2), chunk(buf, 4, k), rs.at[k]).start()
-            wait_bytes(idb.at[4], ri)
-            for j, dx in enumerate((1, RING - 1)):
-                remote(idb.at[4], idb.at[4], t_ix.at[j], ri, at_x(dx)).start()
-
-            @pl.loop(0, CHUNKS)
-            def _(k):
-                wait_bytes(chunk(buf, 4, k), rs.at[k])
-                for j, dx in enumerate((1, RING - 1)):
-                    remote(chunk(buf, 4, k), chunk(buf, 4, k), t_x.at[j], rs.at[k], at_x(dx)).start()
+                pltpu.make_async_copy(chunk_of_block(held, k - CHUNKS // 2), chunk(buf, 4, k), rs.at[k]).start()
 
         for b in range(3):
             wait_bytes(dpiece.at[b], s_piece.at[b])
@@ -259,7 +256,7 @@
         z_rel = lax.rem(z - 2 * (x % 2) + RING, RING)
         steps = ((1, 0), (RING - 1, 0), (0, 1), (0, RING - 1))
         near = [(w, lax.rem(y + dy, RING) * RING + lax.rem(z + dz, RING)) for dy, dz in steps]
-        sources, sends = [], []
+        sources, sends, depths = [], [], []
         for g in range(4):
             h, q = g // 2, g % 2
             y_own = lax.rem(y_rel + 2 * h, RING)
@@ -268,47 +265,74 @@
             flags = [(jnp.int32(mask) >> index) & 1 for mask in CHILDREN]
             if q == 1:
                 flags[2], flags[3] = flags[3], flags[2]
+            depths.append(sum(((jnp.int32(mask) >> index) & 1) << b for b, mask in enumerate(DEPTH)))
             sources.append(index == 0)
             sends.append(flags)
 
-        def pass_on(part, row_recv, row_from_x, tree_recv, x_send, tree_send, to0, to0_send, to0_row, x_odd):
-            @pl.when(x != 0)
-            def _():
-                wait_bytes(part(4), row_recv)
-
-                @pl.when(x == 1 + 2 * x_odd)
-                def _():
-                    remote(part(4), part(4), x_send, row_recv, (5, n)).start()
-
-            remote(part(4), part(4), to0_send(4), to0_row, partner).start()
+        def pass_row(part, recv, x_send, send, to0, to0_send, tree_recv, x_odd):
+            wait_bytes(part(4), recv)
+
+            @pl.when(x == 0)
+            def _():
+                for j, dx in enumerate((1, RING - 1)):
+                    remote(part(4), part(4), x_send.at[j], recv, at_x(dx)).start()
+
+            @pl.when(x == 1 + 2 * x_odd)
+            def _():
+                remote(part(4), part(4), x_send.at[0], recv, (5, n)).start()
+
             for g in range(4):
                 @pl.when(sources[g])
                 def _():
                     for d in range(4):
-                        remote(part(4), part(g), tree_send(g, d), tree_recv(g), near[d]).start()
-
-                @pl.when(jnp.logical_not(sources[g]))
-                def _():
-                    wait_bytes(part(g), tree_recv(g))
-                    for d in range(4):
-                        @pl.when(sends[g][d] == 1)
-                        def _():
-                            remote(part(g), part(g), tree_send(g, d), tree_recv(g), near[d]).start()
-
-                    if g % 2 == 0:
-                        remote(part(g), part(g), to0_send(g), to0(g), partner).start()
-
-        pass_on(
-            lambda g: idb.at[g], ri, None, lambda g: pi.at[g], t_ix.at[0], lambda g, d: t_itree.at[g, d],
-            lambda g: s_to0.at[g], lambda g: t_ito0.at[g], s_to0.at[4], 0,
-        )
-
-        @pl.loop(0, CHUNKS)
-        def _(k):
-            pass_on(
-                lambda g: chunk(buf, g, k), rs.at[k], None, lambda g: ps.at[g, k], t_x.at[0],
-                lambda g, d: t_tree.at[g, d], lambda g: s_to0.at[g + 1], lambda g: t_to0.at[g], s_to0.at[5], k % 2,
-            )
+                        remote(part(4), part(g), send(g, d), tree_recv(g), near[d]).start()
+
+            remote(part(4), part(4), to0_send(4), to0, partner).start()
+
+        def pass_piece(g, part, recv, send, to0, to0_send):
+            wait_bytes(part(g), recv)
+            for d in range(4):
+                @pl.when(sends[g][d] == 1)
+                def _():
+                    remote(part(g), part(g), send(g, d), recv, near[d]).start()
+
+            if g % 2 == 0:
+                remote(part(g), part(g), to0_send(g), to0(g), partner).start()
+
+        @pl.loop(0, CHUNKS + 4 * SKEW)
+        def _(t):
+            @pl.when(t == 0)
+            def _():
+                pass_row(
+                    lambda g: idb.at[g], ri, t_ix, lambda g, d: t_itree.at[g, d], s_to0.at[4],
+                    lambda g: t_ito0.at[g], lambda g: pi.at[g], 0,
+                )
+
+            @pl.when(t < CHUNKS)
+            def _():
+                k = jnp.minimum(t, CHUNKS - 1)
+                pass_row(
+                    lambda g: chunk(buf, g, k), rs.at[k], t_x, lambda g, d: t_tree.at[g, d], s_to0.at[5],
+                    lambda g: t_to0.at[g], lambda g: ps.at[g, k], k % 2,
+                )
+
+            for g in range(4):
+                late = t - SKEW * depths[g]
+
+                @pl.when(jnp.logical_not(sources[g]) & (late == 0))
+                def _():
+                    pass_piece(
+                        g, lambda g: idb.at[g], pi.at[g], lambda g, d: t_itree.at[g, d], lambda g: s_to0.at[g],
+                        lambda g: t_ito0.at[g],
+                    )
+
+                @pl.when(jnp.logical_not(sources[g]) & (late >= 0) & (late < CHUNKS))
+                def _():
+                    k = jnp.minimum(jnp.maximum(late, 0), CHUNKS - 1)
+                    pass_piece(
+                        g, lambda g: chunk(buf, g, k), ps.at[g, k], lambda g, d: t_tree.at[g, d],
+                        lambda g: s_to0.at[g + 1], lambda g: t_to0.at[g],
+                    )
 
         @pl.when(x == 0)
         def _():
@@ -355,147 +379,177 @@
 
 
 def chunk_of_block(blk, k):
-    return blk.at[k // 2, pl.ds((k % 2) * H, H)]
+    return blk.at[k // PARTS, pl.ds((k % PARTS) * PART, PART)]
 
 
 def split(a):
     high = a.astype(jnp.bfloat16)
-    return high, (a - high.astype(F32)).astype(jnp.bfloat16)
+    rest = a - high.astype(F32)
+    middle = rest.astype(jnp.bfloat16)
+    return high, middle, (rest - middle.astype(F32)).astype(jnp.bfloat16)
+
+
+def left_terms(h, m, low):
+    return [h, h, m, h, m, low]
+
+
+def right_terms(h, m, low):
+    return [h, m, h, low, m, h]
+
+
+def stacked_dot(left, right):
+    return lax.dot_general(
+        jnp.concatenate(left, axis=1), jnp.concatenate(right, axis=1),
+        (((1,), (1,)), ((), ())), preferred_element_type=F32,
+    )
 
 
 def local_kernel(
     bmap, idb, blk, buf, ch, out,
-    vb, pan, chv, low_r, low_c, row3, col3, g_ref, s_in, s_out, s_pan, s_ch,
+    vb, pan, chv, parts, inv_parts, prod, where_to, s_in, s_out, s_pan, s_ch,
 ):
     w = lax.axis_index("wide")
     n = lax.axis_index("narrow")
-    x, core = w // 2, w % 2
+    core = w % 2
     slots = blk.shape[0]
-    piece = [jnp.where(n == w + 8 * h, 4, 2 * h + core) for h in range(2)]
-    copies = [
-        pltpu.make_async_copy(ch, chv, s_ch),
-        pltpu.make_async_copy(buf.at[4], pan.at[0], s_pan.at[0]),
-        pltpu.make_async_copy(buf.at[piece[0]], pan.at[1], s_pan.at[1]),
-        pltpu.make_async_copy(buf.at[piece[1]], pan.at[2], s_pan.at[2]),
-    ]
+    slot_of = [jnp.int32(4)] + [jnp.where(n == w + 8 * h, 4, 2 * h + core) for h in range(2)]
+    copies = [pltpu.make_async_copy(ch, chv, s_ch)]
+    for column in range(2):
+        for q in range(3):
+            copies.append(
+                pltpu.make_async_copy(
+                    buf.at[slot_of[q], pl.ds(column * PR, PR)], pan.at[column, pl.ds(q * PR, PR)], s_pan.at[column, q]
+                )
+            )
     for copy in copies:
         copy.start()
-
-    @pl.loop(0, slots)
-    def _(s):
-        pltpu.make_async_copy(blk.at[s], vb.at[s], s_in.at[s]).start()
-
-    for copy in copies:
-        copy.wait()
 
     def find(slot, column, block_row):
         found = jnp.int32(-1)
         for i in range(PR):
-            found = jnp.where(idb[slot, column, i, 0] == block_row, i, found)
+            found = jnp.where(idb[slot, column, 0, i] == block_row, i, found)
         return found
 
-    def store_row(i, value):
-        low_r[i] = value
-        high, rest = split(value)
-        row3[i, :, 0:W] = high
-        row3[i, :, W : 2 * W] = high
-        row3[i, :, 2 * W : 3 * W] = rest
-
-    def store_col(j, value):
-        high, rest = split(value)
-        col3[j, 0:W, :] = high
-        col3[j, W : 2 * W, :] = rest
-        col3[j, 2 * W : 3 * W, :] = high
-
-    @pl.loop(0, PR)
-    def _(i):
-        store_row(i, dot_nt(pan[0, i], chv[1]))
+    @pl.loop(0, slots)
+    def _(s):
+        r, c = bmap[0, s], bmap[1, s]
+        h = (c % 16) // 8
+        i, j = find(4, 1, r), find(jnp.where(h == 0, slot_of[1], slot_of[2]), 1, c)
+        code = jnp.where((c > 1) & (i >= 0) & (j >= 0), i + PR * (j + PR * h), -1)
+        code = jnp.where(c == 0, 32 + find(4, 0, r), jnp.where(c == 1, 32 + i, code))
+        where_to[s] = code
+
+        @pl.when(code < 32)
+        def _():
+            pltpu.make_async_copy(blk.at[s], vb.at[s], s_in.at[s]).start()
+
+    for copy in copies:
+        copy.wait()
+
+    first_inv = split(chv[1])
+    for k in range(3):
+        inv_parts[:, k * W : (k + 1) * W] = first_inv[k]
+    second_inv = split(chv[4])
+    coupling = split(-dot_nn(chv[4], chv[2]))
+    for k in range(3):
+        inv_parts[:, (3 + k) * W : (4 + k) * W] = second_inv[k]
+        inv_parts[:, (6 + k) * W : (7 + k) * W] = coupling[k]
+
+    def inverse(t):
+        return [inv_parts[:, (3 * t + k) * W : (3 * t + k + 1) * W] for k in range(3)]
+
+    @pl.loop(0, 3 * PR // 2)
+    def _(b):
+        old = pan[0, pl.ds(2 * b, 2)].reshape(2 * W, W)
+        value = stacked_dot(left_terms(*split(old)), right_terms(*inverse(0)))
+        pan[0, pl.ds(2 * b, 2)] = value.reshape(2, W, W)
+
+    @pl.loop(0, slots)
+    def _(s):
+        @pl.when(where_to[s] < 0)
+        def _():
+            pltpu.make_async_copy(blk.at[s], vb.at[s], s_in.at[s]).wait()
+            pltpu.make_async_copy(vb.at[s], out.at[s], s_out).start()
+
+    @pl.loop(0, 3 * PR // 2)
+    def _(b):
+        q = b // 2
+        slot = jnp.where(q == 0, slot_of[0], jnp.where(q == 1, slot_of[1], slot_of[2]))
+        firsts = []
+        for d in range(2):
+            block_row = idb[slot, 1, 0, (2 * b + d) % PR]
+            i = find(slot, 0, block_row)
+            value = pan[0, q * PR + jnp.maximum(i, 0)]
+            firsts.append(jnp.where((i >= 0) & (block_row > 0), value, 0.0))
+        first = split(jnp.concatenate(firsts, axis=0))
+        old = split(pan[1, pl.ds(2 * b, 2)].reshape(2 * W, W))
+        value = stacked_dot(
+            left_terms(*old) + left_terms(*first), right_terms(*inverse(1)) + right_terms(*inverse(2))
+        )
+        pan[1, pl.ds(2 * b, 2)] = value.reshape(2, W, W)
+        second = split(value)
+        for k, part in enumerate((first[0], first[1], second[0], second[1])):
+            parts[pl.ds(2 * b, 2), :, k * W : (k + 1) * W] = part.reshape(2, W, W)
+
+    def part(at, count, k):
+        return parts[at, :, k * W : (k + 1) * W].reshape(count * W, W)
 
     @pl.loop(0, 2 * PR)
     def _(j):
-        value = dot_nt(chv[1], pan[1 + j // PR, j % PR])
-        low_c[j] = value
-        store_col(j, value)
-
-    g_ref[...] = dot_nn(chv[4], chv[2])
-
-    @pl.loop(0, PR)
-    def _(i):
-        from_first = find(4, 0, idb[4, 1, i, 0])
-        pan[0, i] = dot_nt(pan[0, PR + i], chv[4])
-
-        @pl.when((from_first >= 0) & (idb[4, 1, i, 0] > 0))
-        def _():
-            pan[0, i] = pan[0, i] - dot_nt(low_r[jnp.maximum(from_first, 0)], g_ref[...])
-
-        store_row(PR + i, pan[0, i])
-
-    @pl.loop(0, 2 * PR)
-    def _(j):
-        h, i = j // PR, j % PR
-        slot = jnp.where(h == 0, piece[0], piece[1])
-        block_row = idb[slot, 1, i, 0]
-        from_first = find(slot, 0, block_row)
-        pan[1 + h, i] = dot_nt(chv[4], pan[1 + h, PR + i])
-
-        @pl.when((from_first >= 0) & (block_row > 0))
-        def _():
-            pan[1 + h, i] = pan[1 + h, i] - dot_nn(g_ref[...], low_c[h * PR + jnp.maximum(from_first, 0)])
-
-        store_col(2 * PR + j, pan[1 + h, i])
+        left = [part(pl.ds(0, PR), PR, k) for k in (0, 0, 1, 2, 2, 3)]
+        right = [part(pl.ds(PR + j, 1), 1, k) for k in (0, 1, 0, 2, 3, 2)]
+        prod[j] = stacked_dot(left, right).reshape(PR, W, W)
 
     @pl.loop(0, slots)
     def _(s):
-        r, c = bmap[s, 0], bmap[s, 1]
-        h = (c % 16) // 8
-        slot = jnp.where(h == 0, piece[0], piece[1])
-        pltpu.make_async_copy(blk.at[s], vb.at[s], s_in.at[s]).wait()
-        for column in range(2):
-            i, j = find(4, column, r), find(slot, column, c)
-
-            @pl.when((r > column) & (c > column) & (i >= 0) & (j >= 0))
-            def _():
-                vb[s] = vb[s] - jnp.dot(
-                    row3[column * PR + jnp.maximum(i, 0)],
-                    col3[column * 2 * PR + h * PR + jnp.maximum(j, 0)],
-                    preferred_element_type=F32,
-                )
-
-            @pl.when((c == column) & (i >= 0))
-            def _():
-                vb[s] = low_r[column * PR + jnp.maximum(i, 0)]
-
-                @pl.when(r == column)
-                def _():
-                    vb[s] = chv[3 * column]
-
-        pltpu.make_async_copy(vb.at[s], out.at[s], s_out).start()
-
-    pltpu.make_async_copy(vb, out, s_out).wait()
+        code = where_to[s]
+
+        @pl.when((code >= 0) & (code < 32))
+        def _():
+            pltpu.make_async_copy(blk.at[s], vb.at[s], s_in.at[s]).wait()
+            vb[s] = vb[s] - prod[jnp.maximum(code, 0) // PR, jnp.maximum(code, 0) % PR]
+
+        @pl.when(code >= 32)
+        def _():
+            r, c = bmap[0, s], bmap[1, s]
+
+            @pl.when(r == c)
+            def _():
+                vb[s] = chv[3 * c]
+
+            @pl.when(r != c)
+            def _():
+                vb[s] = pan[c, code - 32]
+
+        @pl.when(code >= 0)
+        def _():
+            pltpu.make_async_copy(vb.at[s], out.at[s], s_out).start()
+
+    pltpu.make_async_copy(out, out, s_out).wait()
 
 
 def on_device(blocks, block_map):
-    ids = jnp.broadcast_to(jnp.pad(block_map[:PR, 0], (0, G - PR))[:, None], (G, H))
-    anywhere = pl.BlockSpec(memory_space=pl.ANY)
+    ids = block_map.T
+    anywhere = pl.BlockSpec(memory_space=pltpu.HBM)
     dma = pltpu.SemaphoreType.DMA
     vmem = pltpu.VMEM
     buf, idb, ch = pl.pallas_call(
         send_kernel,
         out_shape=[
             jax.ShapeDtypeStruct((5, 2 * PR, W, W), F32),
-            jax.ShapeDtypeStruct((5, 2, G, H), jnp.int32),
+            jax.ShapeDtypeStruct((5, 2) + ids.shape, jnp.int32),
             jax.ShapeDtypeStruct((5, W, W), F32),
         ],
         in_specs=[anywhere, anywhere],
         out_specs=[anywhere, anywhere, anywhere],
         scratch_shapes=[
-            vmem((W, W), F32), vmem((3, ROWS, W), F32), vmem((3, W, W), F32), vmem((5, W, W), F32),
+            vmem((W, W), F32), vmem((3, ROWS, W), F32), vmem((PR, W, W), F32), vmem((3, W, W), F32), vmem((5, W, W), F32),
             vmem((H, H), F32), vmem((H, H), F32), vmem((H, H), F32), vmem((H, H), F32),
             dma((CHUNKS,)), dma((4, CHUNKS)), dma, dma((4,)), dma, dma((3,)), dma((3,)), dma((6,)), dma,
             dma((2,)), dma((4, 4)), dma((2,)), dma((4, 4)), dma((5,)), dma((5,)), dma, dma((3,)), dma((3,)), dma((3,)),
             dma((2,)), dma((2,)),
         ],
-        compiler_params=pltpu.CompilerParams(collective_id=0, has_side_effects=True, vmem_limit_bytes=16 * 2**20),
+        compiler_params=pltpu.CompilerParams(collective_id=0, has_side_effects=True, vmem_limit_bytes=60 * 2**20),
     )(blocks, ids)
     slots = blocks.shape[0]
     return pl.pallas_call(
@@ -506,13 +560,13 @@
         ],
         out_specs=anywhere,
         scratch_shapes=[
-            vmem((slots, W, W), F32), vmem((3, 2 * PR, W, W), F32), vmem((5, W, W), F32),
-            vmem((2 * PR, W, W), F32), vmem((2 * PR, W, W), F32),
-            vmem((2 * PR, W, 3 * W), jnp.bfloat16), vmem((4 * PR, 3 * W, W), jnp.bfloat16), vmem((W, W), F32),
-            dma((slots,)), dma, dma((3,)), dma,
+            vmem((slots, W, W), F32), vmem((2, 3 * PR, W, W), F32), vmem((5, W, W), F32),
+            vmem((3 * PR, W, 4 * W), jnp.bfloat16), vmem((W, 9 * W), jnp.bfloat16), vmem((2 * PR, PR, W, W), F32),
+            pltpu.SMEM((slots,), jnp.int32),
+            dma((slots,)), dma, dma((2, 3)), dma,
         ],
-        compiler_params=pltpu.CompilerParams(vmem_limit_bytes=44 * 2**20),
-    )(block_map, idb, blocks, buf, ch)
+        compiler_params=pltpu.CompilerParams(vmem_limit_bytes=60 * 2**20),
+    )(ids, idb, blocks, buf, ch)
 
 
 def solution(mesh):

time: 536 us -> 84.1 us (0.16)
  Pallas kernels: 526 us -> 83.7 us
  local copies, waits for them, and re-layouts: 9.48 us -> 0 us
    pallas_call x1, Pallas kernels: 493 us -> 58.5 us  [on_device(): pl.pallas_call(send_kernel, out_shape=[jax.ShapeDtypeStruct((5, 2 * PR, W...]
    unnamed x5 -> x0, local copies, waits for them, and re-layouts: 8.72 us -> none
    pallas_call x1, Pallas kernels: 33.7 us -> 25.3 us  [on_device(): pl.pallas_call(local_kernel, out_shape=jax.ShapeDtypeStruct(blocks.shape,...]
where the time goes in v2:
time: 84.1 us; the launch traced here: 83.9 us
  Pallas kernels  83.7 us (100%)
    pallas_call x1, Pallas kernels, on_device(): pl.pallas_call(send_kernel, out_shape=[jax.ShapeDtypeStruct((5, 2 * PR, W...  58.5 us
    pallas_call x1, Pallas kernels, on_device(): pl.pallas_call(local_kernel, out_shape=jax.ShapeDtypeStruct(blocks.shape,...  25.3 us

profile of v2, /device:TPU:5, one launch (start us, length us, event | category | flops | bytes accessed | tf_op | source)
XLA Modules:
  0.0 83.9 jit_solution(2199109794425986483)
XLA Ops:
  0.0 58.5 %shard_map.28 = (f32[5,8,256,256]{3,2,1,0:T(8,128)}, s32[5,2,2,40]{3,2,1,0:T(2,128)}, f32[5,256,256]{2,1,0:T(8,128)}) custom-call(f32[40,256,256]{2,1,0:T(8,128)} %blk.3, s32[2,40]{1,0:T(2,128)} %bitcast.1), custom_call_target="tpu_custom_call" | custom-call | tf_op jit(solution)/shard_map/pallas_call | solution.py:536
  58.5 25.3 %shard_map.29 = f32[40,256,256]{2,1,0:T(8,128)} custom-call(s32[2,40]{1,0:T(2,128)} %bitcast.2, s32[5,2,2,40]{3,2,1,0:T(2,128)} %get-tuple-element.8.idb, f32[40,256,256]{2,1,0:T(8,128)} %blk.3, f32[5,8,256,256]{3,2,1,0:T(8,128)} %get-tuple-element.9.buf, f32[5,256,256]{2,1,0:T(8,128)} %get-tuple-element.10.ch), custom_call_target="tpu_custom_call" | custom-call | tf_op jit(solution)/shard_map/pallas_call | solution.py:555

commit v3 on v2

--- a/solution.py
+++ b/solution.py
@@ -16,7 +16,7 @@
 ROWS = 16
 CHILDREN = (85, 40969, 4097, 32857)
 DEPTH = (23130, 60356, 1056)
-SKEW = 4
+SKEW = 5
 MESH = pl.DeviceIdType.MESH
 HIGHEST = lax.Precision.HIGHEST
 F32 = jnp.float32
@@ -139,21 +139,68 @@
 
     @pl.when(core == 0)
     def _():
+        signal(partner)
+        for dx in range(1, RING):
+            signal((lax.rem(x + dx, RING) * 2, n))
+
         @pl.loop(0, RING * RING)
         def _(i):
-            signal((x * 2 + 1, i))
-
-        pl.semaphore_wait(barrier, 1)
+            @pl.when(i != n)
+            def _():
+                signal((w, i))
+
+        pl.semaphore_wait(barrier, RING * RING + RING - 1)
+
+        def scatter(b, src):
+            @pl.loop(0, RING * RING)
+            def _(i):
+                part = src.at[pl.ds(pl.multiple_of(i * ROWS, ROWS), ROWS)]
+
+                @pl.when(i != n)
+                def _():
+                    remote(part, dpiece.at[b], t_scat.at[b], s_piece.at[b], (w, i)).start()
+
+                @pl.when(i == n)
+                def _():
+                    pltpu.make_async_copy(part, dpiece.at[b], s_piece.at[b]).start()
 
         @pl.when(x == 0)
         def _():
-            @pl.when(n < 2)
-            def _():
-                remote(blk.at[0], dsrc, t_src, s_src, partner).start()
+            @pl.when(n == 0)
+            def _():
+                scatter(0, blk.at[0])
+
+            @pl.when(n == 1)
+            def _():
+                scatter(1, blk.at[0])
 
             remote(idt, idb.at[4, 0], t_first.at[0], ri, partner).start()
             for k in range(CHUNKS // 2):
                 remote(chunk_of_block(blk, k), chunk(buf, 4, k), t_first.at[1], rs.at[k], partner).start()
+
+            @pl.when(n == 1)
+            def _():
+                wait_bytes(dsrc, s_src)
+                scatter(2, dsrc)
+
+        mine = pl.ds(pl.multiple_of(n * ROWS, ROWS), ROWS)
+        for b in range(3):
+            wait_bytes(dpiece.at[b], s_piece.at[b])
+
+            @pl.when(x == 0)
+            def _():
+                for dx in range(1, RING):
+                    remote(dpiece.at[b], dpiece.at[b], t_dx.at[b], s_piece.at[b], (dx * 2, n)).start()
+
+            @pl.loop(0, RING * RING)
+            def _(i):
+                @pl.when(i != n)
+                def _():
+                    remote(dpiece.at[b], dfull.at[b, mine], t_gath.at[b], s_full.at[b], (w, i)).start()
+
+                @pl.when(i == n)
+                def _():
+                    pltpu.make_async_copy(dpiece.at[b], dfull.at[b, mine], s_full.at[b]).start()
 
         wait_bytes(dfull.at[0], s_full.at[0])
         factor_256(dfull.at[0], chv.at[0], chv.at[1], c_ref, u_ref, x_ref, g_ref)
@@ -169,13 +216,24 @@
 
         @pl.when(x == 0)
         def _():
-            @pl.when(n < 2)
-            def _():
-                wait_bytes(dsrc, t_src)
+            for b in range(3):
+                for dx in range(1, RING):
+                    wait_bytes(dpiece.at[b], t_dx.at[b])
+
+            @pl.when(n == 0)
+            def _():
+                wait_bytes(dfull.at[0, pl.ds(0, W - ROWS)], t_scat.at[0])
+
+            @pl.when(n == 1)
+            def _():
+                for b in (1, 2):
+                    wait_bytes(dfull.at[b, pl.ds(0, W - ROWS)], t_scat.at[b])
 
             wait_bytes(idt, t_first.at[0])
             wait_bytes(buf.at[4, pl.ds(0, PR)], t_first.at[1])
 
+        for b in range(3):
+            wait_bytes(dfull.at[b, pl.ds(0, W - ROWS)], t_gath.at[b])
         for h in range(2):
             @pl.when(n != 2 * x + 8 * h)
             def _():
@@ -189,48 +247,20 @@
 
     @pl.when(core == 1)
     def _():
+        steps = ((1, 0), (RING - 1, 0), (0, 1), (0, RING - 1))
+        near = [(w, lax.rem(y + dy, RING) * RING + lax.rem(z + dz, RING)) for dy, dz in steps]
         signal(partner)
         for dx in range(1, RING):
             signal(at_x(dx))
-
-        @pl.loop(0, RING * RING)
-        def _(i):
-            @pl.when(i != n)
-            def _():
-                signal((w, i))
-
-        pl.semaphore_wait(barrier, 2 * RING * RING - 1 + RING - 1)
-
-        def scatter(b, src):
-            @pl.loop(0, RING * RING)
-            def _(i):
-                part = src.at[pl.ds(pl.multiple_of(i * ROWS, ROWS), ROWS)]
-
-                @pl.when(i != n)
-                def _():
-                    remote(part, dpiece.at[b], t_scat.at[b], s_piece.at[b], (w, i)).start()
-
-                @pl.when(i == n)
-                def _():
-                    pltpu.make_async_copy(part, dpiece.at[b], s_piece.at[b]).start()
+        for device in near:
+            signal(device)
+        pl.semaphore_wait(barrier, 1 + RING - 1 + len(near))
 
         @pl.when(x == 0)
         def _():
             @pl.when(n == 1)
             def _():
-                scatter(2, blk.at[0])
-
-            @pl.when(n < 2)
-            def _():
-                wait_bytes(dsrc, s_src)
-
-                @pl.when(n == 0)
-                def _():
-                    scatter(0, dsrc)
-
-                @pl.when(n == 1)
-                def _():
-                    scatter(1, dsrc)
+                remote(blk.at[0], dsrc, t_src, s_src, partner).start()
 
             pltpu.make_async_copy(idt, idb.at[4, 1], ri).start()
             pltpu.make_async_copy(blk.at[pl.ds(0, PR)], held, t_first.at[0]).start()
@@ -238,24 +268,8 @@
             for k in range(CHUNKS // 2, CHUNKS):
                 pltpu.make_async_copy(chunk_of_block(held, k - CHUNKS // 2), chunk(buf, 4, k), rs.at[k]).start()
 
-        for b in range(3):
-            wait_bytes(dpiece.at[b], s_piece.at[b])
-
-            @pl.when(x == 0)
-            def _():
-                for dx in range(1, RING):
-                    remote(dpiece.at[b], dpiece.at[b], t_dx.at[b], s_piece.at[b], at_x(dx)).start()
-
-            mine = pl.ds(pl.multiple_of(n * ROWS, ROWS), ROWS)
-
-            @pl.loop(0, RING * RING)
-            def _(i):
-                remote(dpiece.at[b], dfull.at[b, mine], t_gath.at[b], s_full.at[b], (x * 2, i)).start()
-
         y_rel = lax.rem(y - x // 2 + RING, RING)
         z_rel = lax.rem(z - 2 * (x % 2) + RING, RING)
-        steps = ((1, 0), (RING - 1, 0), (0, 1), (0, RING - 1))
-        near = [(w, lax.rem(y + dy, RING) * RING + lax.rem(z + dz, RING)) for dy, dz in steps]
         sources, sends, depths = [], [], []
         for g in range(4):
             h, q = g // 2, g % 2
@@ -269,88 +283,93 @@
             sources.append(index == 0)
             sends.append(flags)
 
-        def pass_row(part, recv, x_send, send, to0, to0_send, tree_recv, x_odd):
-            wait_bytes(part(4), recv)
+        out_any, out_g, out_slot, out_lag = [], [], [], []
+        for d in range(4):
+            here = [jnp.where(sources[g], 1, sends[g][d]) for g in range(4)]
+            out_any.append(sum(here) > 0)
+            out_g.append(sum(g * here[g] for g in range(4)))
+            out_slot.append(sum(jnp.where(sources[g], 4, g) * here[g] for g in range(4)))
+            out_lag.append(sum(SKEW * depths[g] * here[g] for g in range(4)))
+        lags = [jnp.where(sources[g], CHUNKS + 4 * SKEW, SKEW * depths[g]) for g in range(4)]
+
+        def pass_row(part, recv, x_send, x_odd):
+            wait_bytes(part, recv)
 
             @pl.when(x == 0)
             def _():
                 for j, dx in enumerate((1, RING - 1)):
-                    remote(part(4), part(4), x_send.at[j], recv, at_x(dx)).start()
+                    remote(part, part, x_send.at[j], recv, at_x(dx)).start()
 
             @pl.when(x == 1 + 2 * x_odd)
             def _():
-                remote(part(4), part(4), x_send.at[0], recv, (5, n)).start()
-
-            for g in range(4):
-                @pl.when(sources[g])
-                def _():
-                    for d in range(4):
-                        remote(part(4), part(g), send(g, d), tree_recv(g), near[d]).start()
-
-            remote(part(4), part(4), to0_send(4), to0, partner).start()
-
-        def pass_piece(g, part, recv, send, to0, to0_send):
-            wait_bytes(part(g), recv)
-            for d in range(4):
-                @pl.when(sends[g][d] == 1)
-                def _():
-                    remote(part(g), part(g), send(g, d), recv, near[d]).start()
-
-            if g % 2 == 0:
-                remote(part(g), part(g), to0_send(g), to0(g), partner).start()
+                remote(part, part, x_send.at[0], recv, (5, n)).start()
+
+        def block_over(slot, k, send, recv):
+            @pl.when(k % PARTS == PARTS - 1)
+            def _():
+                block = buf.at[slot, k // PARTS]
+                remote(block, block, send, recv, partner).start()
 
         @pl.loop(0, CHUNKS + 4 * SKEW)
         def _(t):
-            @pl.when(t == 0)
-            def _():
-                pass_row(
-                    lambda g: idb.at[g], ri, t_ix, lambda g, d: t_itree.at[g, d], s_to0.at[4],
-                    lambda g: t_ito0.at[g], lambda g: pi.at[g], 0,
-                )
-
             @pl.when(t < CHUNKS)
             def _():
                 k = jnp.minimum(t, CHUNKS - 1)
-                pass_row(
-                    lambda g: chunk(buf, g, k), rs.at[k], t_x, lambda g, d: t_tree.at[g, d], s_to0.at[5],
-                    lambda g: t_to0.at[g], lambda g: ps.at[g, k], k % 2,
-                )
+
+                @pl.when(t == 0)
+                def _():
+                    pass_row(idb.at[4], ri, t_ix, 0)
+                    remote(idb.at[4], idb.at[4], t_ito0.at[4], s_to0.at[4], partner).start()
+
+                pass_row(chunk(buf, 4, k), rs.at[k], t_x, k % 2)
 
             for g in range(4):
-                late = t - SKEW * depths[g]
-
-                @pl.when(jnp.logical_not(sources[g]) & (late == 0))
-                def _():
-                    pass_piece(
-                        g, lambda g: idb.at[g], pi.at[g], lambda g, d: t_itree.at[g, d], lambda g: s_to0.at[g],
-                        lambda g: t_ito0.at[g],
-                    )
-
-                @pl.when(jnp.logical_not(sources[g]) & (late >= 0) & (late < CHUNKS))
+                late = t - lags[g]
+
+                @pl.when((late >= 0) & (late < CHUNKS))
                 def _():
                     k = jnp.minimum(jnp.maximum(late, 0), CHUNKS - 1)
-                    pass_piece(
-                        g, lambda g: chunk(buf, g, k), ps.at[g, k], lambda g, d: t_tree.at[g, d],
-                        lambda g: s_to0.at[g + 1], lambda g: t_to0.at[g],
-                    )
+                    wait_bytes(chunk(buf, g, k), ps.at[g, k])
+
+                    @pl.when(late == 0)
+                    def _():
+                        wait_bytes(idb.at[g], pi.at[g])
+                        if g % 2 == 0:
+                            remote(idb.at[g], idb.at[g], t_ito0.at[g], s_to0.at[g], partner).start()
+
+            for d in range(4):
+                late = t - out_lag[d]
+
+                @pl.when(out_any[d] & (late >= 0) & (late < CHUNKS))
+                def _():
+                    k = jnp.minimum(jnp.maximum(late, 0), CHUNKS - 1)
+                    g, slot = out_g[d], out_slot[d]
+
+                    @pl.when(late == 0)
+                    def _():
+                        remote(idb.at[slot], idb.at[g], t_itree.at[d], pi.at[g], near[d]).start()
+
+                    remote(chunk(buf, slot, k), chunk(buf, g, k), t_tree.at[d], ps.at[g, k], near[d]).start()
+
+            @pl.when(t < CHUNKS)
+            def _():
+                block_over(4, jnp.minimum(t, CHUNKS - 1), t_to0.at[4], s_to0.at[5])
+
+            for g in (0, 2):
+                late = t - lags[g]
+
+                @pl.when((late >= 0) & (late < CHUNKS))
+                def _():
+                    block_over(g, jnp.minimum(jnp.maximum(late, 0), CHUNKS - 1), t_to0.at[g], s_to0.at[g + 1])
 
         @pl.when(x == 0)
         def _():
             for j in range(2):
                 wait_bytes(idb.at[4], t_ix.at[j])
                 wait_bytes(buf.at[4], t_x.at[j])
-            for b in range(3):
-                for dx in range(1, RING):
-                    wait_bytes(dpiece.at[b], t_dx.at[b])
-
-            @pl.when(n == 0)
-            def _():
-                wait_bytes(dfull.at[0, pl.ds(0, W - ROWS)], t_scat.at[0])
-
             @pl.when(n == 1)
             def _():
-                for b in (1, 2):
-                    wait_bytes(dfull.at[b, pl.ds(0, W - ROWS)], t_scat.at[b])
+                wait_bytes(dsrc, t_src)
 
         @pl.when(x == 1)
         def _():
@@ -360,14 +379,13 @@
         def _():
             wait_bytes(buf.at[4, pl.ds(0, PR)], t_x.at[0])
 
-        for b in range(3):
-            wait_bytes(dfull.at[b], t_gath.at[b])
+        for d in range(4):
+            @pl.when(out_any[d])
+            def _():
+                wait_bytes(idb.at[0], t_itree.at[d])
+                wait_bytes(buf.at[0], t_tree.at[d])
+
         for g in range(4):
-            for d in range(4):
-                @pl.when(sources[g] | (sends[g][d] == 1))
-                def _():
-                    wait_bytes(idb.at[g], t_itree.at[g, d])
-                    wait_bytes(buf.at[g], t_tree.at[g, d])
             if g % 2 == 0:
                 @pl.when(jnp.logical_not(sources[g]))
                 def _():
@@ -406,7 +424,7 @@
 
 def local_kernel(
     bmap, idb, blk, buf, ch, out,
-    vb, pan, chv, parts, inv_parts, prod, where_to, s_in, s_out, s_pan, s_ch,
+    vb, pan, chv, parts, inv_parts, prod, where_to, slot_for, s_in, s_out, s_pan, s_ch,
 ):
     w = lax.axis_index("wide")
     n = lax.axis_index("narrow")
@@ -430,20 +448,29 @@
             found = jnp.where(idb[slot, column, 0, i] == block_row, i, found)
         return found
 
+    @pl.loop(0, 2 * PR * PR)
+    def _(pair):
+        slot_for[pair] = -1
+
     @pl.loop(0, slots)
     def _(s):
         r, c = bmap[0, s], bmap[1, s]
         h = (c % 16) // 8
         i, j = find(4, 1, r), find(jnp.where(h == 0, slot_of[1], slot_of[2]), 1, c)
-        code = jnp.where((c > 1) & (i >= 0) & (j >= 0), i + PR * (j + PR * h), -1)
+        updated = (c > 1) & (i >= 0) & (j >= 0)
+        code = jnp.where(updated, i + PR * (j + PR * h), -1)
         code = jnp.where(c == 0, 32 + find(4, 0, r), jnp.where(c == 1, 32 + i, code))
         where_to[s] = code
 
+        @pl.when(updated)
+        def _():
+            slot_for[jnp.maximum(code, 0)] = s
+
         @pl.when(code < 32)
         def _():
             pltpu.make_async_copy(blk.at[s], vb.at[s], s_in.at[s]).start()
 
-    for copy in copies:
+    for copy in copies[:4]:
         copy.wait()
 
     first_inv = split(chv[1])
@@ -463,6 +490,9 @@
         old = pan[0, pl.ds(2 * b, 2)].reshape(2 * W, W)
         value = stacked_dot(left_terms(*split(old)), right_terms(*inverse(0)))
         pan[0, pl.ds(2 * b, 2)] = value.reshape(2, W, W)
+
+    for copy in copies[4:]:
+        copy.wait()
 
     @pl.loop(0, slots)
     def _(s):
@@ -494,21 +524,13 @@
     def part(at, count, k):
         return parts[at, :, k * W : (k + 1) * W].reshape(count * W, W)
 
-    @pl.loop(0, 2 * PR)
-    def _(j):
-        left = [part(pl.ds(0, PR), PR, k) for k in (0, 0, 1, 2, 2, 3)]
-        right = [part(pl.ds(PR + j, 1), 1, k) for k in (0, 1, 0, 2, 3, 2)]
-        prod[j] = stacked_dot(left, right).reshape(PR, W, W)
-
-    @pl.loop(0, slots)
+    def leave(s):
+        pltpu.make_async_copy(vb.at[s], out.at[s], s_out).start()
+
+    @pl.loop(0, PR)
     def _(s):
         code = where_to[s]
 
-        @pl.when((code >= 0) & (code < 32))
-        def _():
-            pltpu.make_async_copy(blk.at[s], vb.at[s], s_in.at[s]).wait()
-            vb[s] = vb[s] - prod[jnp.maximum(code, 0) // PR, jnp.maximum(code, 0) % PR]
-
         @pl.when(code >= 32)
         def _():
             r, c = bmap[0, s], bmap[1, s]
@@ -521,9 +543,25 @@
             def _():
                 vb[s] = pan[c, code - 32]
 
-        @pl.when(code >= 0)
-        def _():
-            pltpu.make_async_copy(vb.at[s], out.at[s], s_out).start()
+            leave(s)
+
+    @pl.loop(0, 2 * PR * PR // 2)
+    def _(t):
+        j, half = t // (PR // 2), t % (PR // 2)
+        held = [slot_for[PR * j + 2 * half + d] for d in range(2)]
+
+        @pl.when((held[0] >= 0) | (held[1] >= 0))
+        def _():
+            left = [part(pl.ds(2 * half, 2), 2, k) for k in (0, 0, 1, 2, 2, 3)]
+            right = [part(pl.ds(PR + j, 1), 1, k) for k in (0, 1, 0, 2, 3, 2)]
+            prod[...] = stacked_dot(left, right).reshape(2, W, W)
+            for d in range(2):
+                @pl.when(held[d] >= 0)
+                def _():
+                    s = jnp.maximum(held[d], 0)
+                    pltpu.make_async_copy(blk.at[s], vb.at[s], s_in.at[s]).wait()
+                    vb[s] = vb[s] - prod[d]
+                    leave(s)
 
     pltpu.make_async_copy(out, out, s_out).wait()
 
@@ -546,7 +584,7 @@
             vmem((W, W), F32), vmem((3, ROWS, W), F32), vmem((PR, W, W), F32), vmem((3, W, W), F32), vmem((5, W, W), F32),
             vmem((H, H), F32), vmem((H, H), F32), vmem((H, H), F32), vmem((H, H), F32),
             dma((CHUNKS,)), dma((4, CHUNKS)), dma, dma((4,)), dma, dma((3,)), dma((3,)), dma((6,)), dma,
-            dma((2,)), dma((4, 4)), dma((2,)), dma((4, 4)), dma((5,)), dma((5,)), dma, dma((3,)), dma((3,)), dma((3,)),
+            dma((2,)), dma((4,)), dma((2,)), dma((4,)), dma((5,)), dma((5,)), dma, dma((3,)), dma((3,)), dma((3,)),
             dma((2,)), dma((2,)),
         ],
         compiler_params=pltpu.CompilerParams(collective_id=0, has_side_effects=True, vmem_limit_bytes=60 * 2**20),
@@ -561,8 +599,8 @@
         out_specs=anywhere,
         scratch_shapes=[
             vmem((slots, W, W), F32), vmem((2, 3 * PR, W, W), F32), vmem((5, W, W), F32),
-            vmem((3 * PR, W, 4 * W), jnp.bfloat16), vmem((W, 9 * W), jnp.bfloat16), vmem((2 * PR, PR, W, W), F32),
-            pltpu.SMEM((slots,), jnp.int32),
+            vmem((3 * PR, W, 4 * W), jnp.bfloat16), vmem((W, 9 * W), jnp.bfloat16), vmem((2, W, W), F32),
+            pltpu.SMEM((slots,), jnp.int32), pltpu.SMEM((2 * PR * PR,), jnp.int32),
             dma((slots,)), dma, dma((2, 3)), dma,
         ],
         compiler_params=pltpu.CompilerParams(vmem_limit_bytes=60 * 2**20),

time: 84.1 us -> 80.8 us (0.961)
  Pallas kernels: 83.7 us -> 80.4 us
    pallas_call x1, Pallas kernels: 58.5 us -> 55.1 us  [on_device(): pl.pallas_call(send_kernel, out_shape=[jax.ShapeDtypeStruct((5, 2 * PR, W...]
where the time goes in v3:
time: 80.8 us; the launch traced here: 80.6 us
  Pallas kernels  80.4 us (100%)
    pallas_call x1, Pallas kernels, on_device(): pl.pallas_call(send_kernel, out_shape=[jax.ShapeDtypeStruct((5, 2 * PR, W...  55.1 us
    pallas_call x1, Pallas kernels, on_device(): pl.pallas_call(local_kernel, out_shape=jax.ShapeDtypeStruct(blocks.shape,...  25.3 us

profile of v3, /device:TPU:5, one launch (start us, length us, event | category | flops | bytes accessed | tf_op | source)
XLA Modules:
  0.0 80.6 jit_solution(2926961055959370151)
XLA Ops:
  0.0 55.1 %shard_map.28 = (f32[5,8,256,256]{3,2,1,0:T(8,128)}, s32[5,2,2,40]{3,2,1,0:T(2,128)}, f32[5,256,256]{2,1,0:T(8,128)}) custom-call(f32[40,256,256]{2,1,0:T(8,128)} %blk.3, s32[2,40]{1,0:T(2,128)} %bitcast.1), custom_call_target="tpu_custom_call" | custom-call | tf_op jit(solution)/shard_map/pallas_call | solution.py:574
  55.2 25.3 %shard_map.29 = f32[40,256,256]{2,1,0:T(8,128)} custom-call(s32[2,40]{1,0:T(2,128)} %bitcast.2, s32[5,2,2,40]{3,2,1,0:T(2,128)} %get-tuple-element.8.idb, f32[40,256,256]{2,1,0:T(8,128)} %blk.3, f32[5,8,256,256]{3,2,1,0:T(8,128)} %get-tuple-element.9.buf, f32[5,256,256]{2,1,0:T(8,128)} %get-tuple-element.10.ch), custom_call_target="tpu_custom_call" | custom-call | tf_op jit(solution)/shard_map/pallas_call | solution.py:593

commit v4 on v3

--- a/solution.py
+++ b/solution.py
@@ -210,6 +210,7 @@
         wait_bytes(dfull.at[2], s_full.at[2])
         dfull[2] = dfull[2] - dot_nt(l10, l10)
         factor_256(dfull.at[2], chv.at[3], chv.at[4], c_ref, u_ref, x_ref, g_ref)
+        chv[5] = -dot_nn(chv[4], chv[2])
         remote(chv, ch, t_ch.at[0], s_ch, partner).start()
         own = pltpu.make_async_copy(chv, ch, t_ch.at[1])
         own.start()
@@ -442,10 +443,12 @@
     for copy in copies:
         copy.start()
 
-    def find(slot, column, block_row):
+    ids = [[[idb[slot_of[q], column, 0, i] for i in range(PR)] for q in range(3)] for column in range(2)]
+
+    def find(rows, block_row):
         found = jnp.int32(-1)
-        for i in range(PR):
-            found = jnp.where(idb[slot, column, 0, i] == block_row, i, found)
+        for i, held_row in enumerate(rows):
+            found = jnp.where(held_row == block_row, i, found)
         return found
 
     @pl.loop(0, 2 * PR * PR)
@@ -455,11 +458,10 @@
     @pl.loop(0, slots)
     def _(s):
         r, c = bmap[0, s], bmap[1, s]
-        h = (c % 16) // 8
-        i, j = find(4, 1, r), find(jnp.where(h == 0, slot_of[1], slot_of[2]), 1, c)
+        i, j = find(ids[1][0], r), find(ids[1][1] + ids[1][2], c)
         updated = (c > 1) & (i >= 0) & (j >= 0)
-        code = jnp.where(updated, i + PR * (j + PR * h), -1)
-        code = jnp.where(c == 0, 32 + find(4, 0, r), jnp.where(c == 1, 32 + i, code))
+        code = jnp.where(updated, i + PR * j, -1)
+        code = jnp.where(c == 0, 32 + find(ids[0][0], r), jnp.where(c == 1, 32 + i, code))
         where_to[s] = code
 
         @pl.when(updated)
@@ -477,7 +479,7 @@
     for k in range(3):
         inv_parts[:, k * W : (k + 1) * W] = first_inv[k]
     second_inv = split(chv[4])
-    coupling = split(-dot_nn(chv[4], chv[2]))
+    coupling = split(chv[5])
     for k in range(3):
         inv_parts[:, (3 + k) * W : (4 + k) * W] = second_inv[k]
         inv_parts[:, (6 + k) * W : (7 + k) * W] = coupling[k]
@@ -485,8 +487,7 @@
     def inverse(t):
         return [inv_parts[:, (3 * t + k) * W : (3 * t + k + 1) * W] for k in range(3)]
 
-    @pl.loop(0, 3 * PR // 2)
-    def _(b):
+    for b in range(3 * PR // 2):
         old = pan[0, pl.ds(2 * b, 2)].reshape(2 * W, W)
         value = stacked_dot(left_terms(*split(old)), right_terms(*inverse(0)))
         pan[0, pl.ds(2 * b, 2)] = value.reshape(2, W, W)
@@ -494,21 +495,12 @@
     for copy in copies[4:]:
         copy.wait()
 
-    @pl.loop(0, slots)
-    def _(s):
-        @pl.when(where_to[s] < 0)
-        def _():
-            pltpu.make_async_copy(blk.at[s], vb.at[s], s_in.at[s]).wait()
-            pltpu.make_async_copy(vb.at[s], out.at[s], s_out).start()
-
-    @pl.loop(0, 3 * PR // 2)
-    def _(b):
+    for b in range(3 * PR // 2):
         q = b // 2
-        slot = jnp.where(q == 0, slot_of[0], jnp.where(q == 1, slot_of[1], slot_of[2]))
         firsts = []
         for d in range(2):
-            block_row = idb[slot, 1, 0, (2 * b + d) % PR]
-            i = find(slot, 0, block_row)
+            block_row = ids[1][q][(2 * b + d) % PR]
+            i = find(ids[0][q], block_row)
             value = pan[0, q * PR + jnp.maximum(i, 0)]
             firsts.append(jnp.where((i >= 0) & (block_row > 0), value, 0.0))
         first = split(jnp.concatenate(firsts, axis=0))
@@ -521,6 +513,13 @@
         for k, part in enumerate((first[0], first[1], second[0], second[1])):
             parts[pl.ds(2 * b, 2), :, k * W : (k + 1) * W] = part.reshape(2, W, W)
 
+    @pl.loop(0, slots)
+    def _(s):
+        @pl.when(where_to[s] < 0)
+        def _():
+            pltpu.make_async_copy(blk.at[s], vb.at[s], s_in.at[s]).wait()
+            pltpu.make_async_copy(vb.at[s], out.at[s], s_out).start()
+
     def part(at, count, k):
         return parts[at, :, k * W : (k + 1) * W].reshape(count * W, W)
 
@@ -576,12 +575,12 @@
         out_shape=[
             jax.ShapeDtypeStruct((5, 2 * PR, W, W), F32),
             jax.ShapeDtypeStruct((5, 2) + ids.shape, jnp.int32),
-            jax.ShapeDtypeStruct((5, W, W), F32),
+            jax.ShapeDtypeStruct((6, W, W), F32),
         ],
         in_specs=[anywhere, anywhere],
         out_specs=[anywhere, anywhere, anywhere],
         scratch_shapes=[
-            vmem((W, W), F32), vmem((3, ROWS, W), F32), vmem((PR, W, W), F32), vmem((3, W, W), F32), vmem((5, W, W), F32),
+            vmem((W, W), F32), vmem((3, ROWS, W), F32), vmem((PR, W, W), F32), vmem((3, W, W), F32), vmem((6, W, W), F32),
             vmem((H, H), F32), vmem((H, H), F32), vmem((H, H), F32), vmem((H, H), F32),
             dma((CHUNKS,)), dma((4, CHUNKS)), dma, dma((4,)), dma, dma((3,)), dma((3,)), dma((6,)), dma,
             dma((2,)), dma((4,)), dma((2,)), dma((4,)), dma((5,)), dma((5,)), dma, dma((3,)), dma((3,)), dma((3,)),
@@ -598,7 +597,7 @@
         ],
         out_specs=anywhere,
         scratch_shapes=[
-            vmem((slots, W, W), F32), vmem((2, 3 * PR, W, W), F32), vmem((5, W, W), F32),
+            vmem((slots, W, W), F32), vmem((2, 3 * PR, W, W), F32), vmem((6, W, W), F32),
             vmem((3 * PR, W, 4 * W), jnp.bfloat16), vmem((W, 9 * W), jnp.bfloat16), vmem((2, W, W), F32),
             pltpu.SMEM((slots,), jnp.int32), pltpu.SMEM((2 * PR * PR,), jnp.int32),
             dma((slots,)), dma, dma((2, 3)), dma,

time: 80.8 us -> 76.5 us (0.947)
  the two profiles are of different devices: /device:TPU:5 before, /device:TPU:37 now
where the time goes in v4:
time: 76.5 us; the launch traced here: 76.3 us
  Pallas kernels  76.1 us (99%)
    pallas_call x1, Pallas kernels, on_device(): pl.pallas_call(send_kernel, out_shape=[jax.ShapeDtypeStruct((5, 2 * PR, W...  54.4 us
    pallas_call x1, Pallas kernels, on_device(): pl.pallas_call(local_kernel, out_shape=jax.ShapeDtypeStruct(blocks.shape,...  21.6 us

profile of v4, /device:TPU:37, one launch (start us, length us, event | category | flops | bytes accessed | tf_op | source)
XLA Modules:
  0.0 76.3 jit_solution(16013564766304483999)
XLA Ops:
  0.0 54.4 %shard_map.28 = (f32[5,8,256,256]{3,2,1,0:T(8,128)}, s32[5,2,2,40]{3,2,1,0:T(2,128)}, f32[6,256,256]{2,1,0:T(8,128)}) custom-call(f32[40,256,256]{2,1,0:T(8,128)} %blk.3, s32[2,40]{1,0:T(2,128)} %bitcast.1), custom_call_target="tpu_custom_call" | custom-call | tf_op jit(solution)/shard_map/pallas_call | solution.py:573
  54.4 21.6 %shard_map.29 = f32[40,256,256]{2,1,0:T(8,128)} custom-call(s32[2,40]{1,0:T(2,128)} %bitcast.2, s32[5,2,2,40]{3,2,1,0:T(2,128)} %get-tuple-element.8.idb, f32[40,256,256]{2,1,0:T(8,128)} %blk.3, f32[5,8,256,256]{3,2,1,0:T(8,128)} %get-tuple-element.9.buf, f32[6,256,256]{2,1,0:T(8,128)} %get-tuple-element.10.ch), custom_call_target="tpu_custom_call" | custom-call | tf_op jit(solution)/shard_map/pallas_call | solution.py:592

commit v5 on v4

--- a/solution.py
+++ b/solution.py
@@ -549,18 +549,26 @@
         j, half = t // (PR // 2), t % (PR // 2)
         held = [slot_for[PR * j + 2 * half + d] for d in range(2)]
 
-        @pl.when((held[0] >= 0) | (held[1] >= 0))
-        def _():
-            left = [part(pl.ds(2 * half, 2), 2, k) for k in (0, 0, 1, 2, 2, 3)]
+        def update(first, count):
+            left = [part(pl.ds(2 * half + first, count), count, k) for k in (0, 0, 1, 2, 2, 3)]
             right = [part(pl.ds(PR + j, 1), 1, k) for k in (0, 1, 0, 2, 3, 2)]
-            prod[...] = stacked_dot(left, right).reshape(2, W, W)
-            for d in range(2):
-                @pl.when(held[d] >= 0)
-                def _():
-                    s = jnp.maximum(held[d], 0)
-                    pltpu.make_async_copy(blk.at[s], vb.at[s], s_in.at[s]).wait()
-                    vb[s] = vb[s] - prod[d]
-                    leave(s)
+            prod[0:count] = stacked_dot(left, right).reshape(count, W, W)
+            for d in range(count):
+                s = jnp.maximum(held[first] if count == 1 else held[d], 0)
+                pltpu.make_async_copy(blk.at[s], vb.at[s], s_in.at[s]).wait()
+                vb[s] = vb[s] - prod[d]
+                leave(s)
+
+        both = (held[0] >= 0) & (held[1] >= 0)
+
+        @pl.when(both)
+        def _():
+            update(0, 2)
+
+        for d in range(2):
+            @pl.when((held[d] >= 0) & jnp.logical_not(both))
+            def _():
+                update(d, 1)
 
     pltpu.make_async_copy(out, out, s_out).wait()
 

time: 76.5 us -> 76.1 us (level)
  the two profiles are of different devices: /device:TPU:37 before, /device:TPU:5 now
where the time goes in v5:
time: 76.1 us; the launch traced here: 75.7 us
  Pallas kernels  75.6 us (99%)
    pallas_call x1, Pallas kernels, on_device(): pl.pallas_call(send_kernel, out_shape=[jax.ShapeDtypeStruct((5, 2 * PR, W...  55.1 us
    pallas_call x1, Pallas kernels, on_device(): pl.pallas_call(local_kernel, out_shape=jax.ShapeDtypeStruct(blocks.shape,...  20.4 us

profile of v5, /device:TPU:5, one launch (start us, length us, event | category | flops | bytes accessed | tf_op | source)
XLA Modules:
  0.0 75.7 jit_solution(6102224182198530441)
XLA Ops:
  0.0 55.1 %shard_map.28 = (f32[5,8,256,256]{3,2,1,0:T(8,128)}, s32[5,2,2,40]{3,2,1,0:T(2,128)}, f32[6,256,256]{2,1,0:T(8,128)}) custom-call(f32[40,256,256]{2,1,0:T(8,128)} %blk.3, s32[2,40]{1,0:T(2,128)} %bitcast.1), custom_call_target="tpu_custom_call" | custom-call | tf_op jit(solution)/shard_map/pallas_call | solution.py:581
  55.2 20.4 %shard_map.29 = f32[40,256,256]{2,1,0:T(8,128)} custom-call(s32[2,40]{1,0:T(2,128)} %bitcast.2, s32[5,2,2,40]{3,2,1,0:T(2,128)} %get-tuple-element.8.idb, f32[40,256,256]{2,1,0:T(8,128)} %blk.3, f32[5,8,256,256]{3,2,1,0:T(8,128)} %get-tuple-element.9.buf, f32[6,256,256]{2,1,0:T(8,128)} %get-tuple-element.10.ch), custom_call_target="tpu_custom_call" | custom-call | tf_op jit(solution)/shard_map/pallas_call | solution.py:600
